TPU v7x, 256 devices: a whole 4x4x8 slice. The times are simulated.
256 devices in a mesh: dp: 32 (over x, z_hi, core), ctx: 8 (over y, z_lo).
Axes of the slice: x: 4, y: 4, z: 8 (z_hi: 4, z_lo: 2; z = z_hi * 2 + z_lo), core: 2. Of those that a mesh axis runs over, the one named last changes fastest.
Arguments:
- queries: bfloat16 [131072, 1024], P(('dp', 'ctx')), may hold values from -6 to 6
- keys_values: bfloat16 [131072, 1, 2, 128], P(('dp', 'ctx')), may hold values from -6 to 6
- routing: int32 [131072, 2], P(('dp', 'ctx')), may hold values from 0 to 511, as said below
- documents: int32 [131072], P(('dp', 'ctx')), may hold values from 0 to 131071, as said below
Outputs:
- attended: bfloat16 [131072, 1024], P(('dp', 'ctx'))
Inputs may be any that keep to these rules, and one draw needn't show every extreme that they name: routing[r, 0] is the packed sequence and routing[r, 1] the position inside the 512-token block (the block at the owner's index along ctx) to which owner row r goes; every position is filled exactly once. Each aligned block of 32 rows of one owner goes, in order, to 32 consecutive positions of one destination, and different blocks of one owner go to different destinations. `documents`: A token's document id is 4096 times its packed sequence plus the position in that sequence at which its document begins; in every draw some sequence other than the last is one whole document, and every other sequence ends with a one-token document.
All inputs are finite; a program needn't handle non-finite values.
Results may differ from a plain program's by a relative error of at most 0.0045.
Values may be sent and summed in bfloat16 or wider, within the bound.
A program may use at most 64 MiB of HBM per device.

v0:
```python
import math

import jax
import jax.numpy as jnp
from jax import lax
from jax.sharding import PartitionSpec as P


def attend_rows(local_q, local_kv, local_doc):
    rows_dev = local_q.shape[0]
    groups = local_q.shape[1]
    head_dim = local_kv.shape[2] // 2
    per_group = local_q.shape[2] // head_dim
    query_heads = local_q.reshape(rows_dev, groups, per_group, head_dim)
    query_pos = lax.axis_index("ctx") * rows_dev + jnp.arange(rows_dev, dtype=jnp.int32)
    factor = 1.0 / math.sqrt(head_dim)

    def update(state_now, block_kv, block_doc, begin_at):
        width = block_kv.shape[0]
        key_pos = begin_at + jnp.arange(width, dtype=jnp.int32)
        allowed = (local_doc[:, None] == block_doc[None, :]) & (
            key_pos[None, :] <= query_pos[:, None]
        )
        wide_mask = allowed[:, None, None, :]
        peaks, totals, mixed = state_now
        scores = (
            jnp.einsum(
                "tgqd,kgd->tgqk",
                query_heads,
                block_kv[:, :, :head_dim],
                preferred_element_type=jnp.float32,
            )
            * factor
        )
        scores = jnp.where(wide_mask, scores, -1e30)
        new_peaks = jnp.maximum(peaks, jnp.max(scores, axis=-1))
        weights = jnp.where(wide_mask, jnp.exp(scores - new_peaks[..., None]), 0.0)
        decay = jnp.exp(peaks - new_peaks)
        new_totals = totals * decay + jnp.sum(weights, axis=-1)
        product = jnp.einsum(
            "tgqk,kgd->tgqd",
            weights.astype(jnp.bfloat16),
            block_kv[:, :, head_dim:],
            preferred_element_type=jnp.float32,
        )
        return (new_peaks, new_totals, mixed * decay[..., None] + product)

    initial = (
        jnp.full((rows_dev, groups, per_group), -1e30, jnp.float32),
        jnp.zeros((rows_dev, groups, per_group), jnp.float32),
        jnp.zeros((rows_dev, groups, per_group, head_dim), jnp.float32),
    )
    block_kv = lax.all_gather(local_kv, "ctx", axis=0, tiled=True)
    block_doc = lax.all_gather(local_doc, "ctx", axis=0, tiled=True)
    width = block_kv.shape[0]
    count = width // rows_dev
    split_kv = block_kv.reshape(count, rows_dev, groups, 2 * head_dim)
    split_doc = block_doc.reshape(count, rows_dev)
    offsets = rows_dev * jnp.arange(count, dtype=jnp.int32)

    def step(state_in, parts):
        return (update(state_in, parts[0], parts[1], parts[2]), None)

    state_out, unused = lax.scan(step, initial, (split_kv, split_doc, offsets))
    peaks, totals, mixed = state_out
    result = mixed / totals[..., None]
    return result.reshape(rows_dev, groups, per_group * head_dim).astype(jnp.bfloat16)


def local(queries, keys_values, routing, documents):
    rows_dev = queries.shape[0]
    owners = lax.axis_size("dp")
    capacity = 2 * rows_dev // owners
    kv_heads = keys_values.shape[1]
    head_dim = keys_values.shape[3]
    full_width = queries.shape[1]
    group_width = full_width // kv_heads
    buckets = routing[:, 0] * capacity + jnp.arange(rows_dev, dtype=jnp.int32) % capacity
    send_q = jnp.zeros((owners * capacity, full_width), jnp.bfloat16).at[buckets].set(queries)
    send_kv = (
        jnp.zeros((owners * capacity, kv_heads, 2 * head_dim), jnp.bfloat16)
        .at[buckets]
        .set(keys_values.reshape(rows_dev, kv_heads, 2 * head_dim))
    )
    empty_labels = jnp.stack(
        [
            jnp.full((owners * capacity,), rows_dev, jnp.int32),
            jnp.full((owners * capacity,), -1, jnp.int32),
        ],
        axis=1,
    )
    labels = empty_labels.at[buckets].set(jnp.stack([routing[:, 1], documents], axis=1))
    parcel_q = send_q.reshape(owners, capacity, kv_heads, group_width)
    parcel_kv = send_kv.reshape(owners, capacity, kv_heads, 2 * head_dim)
    parcel_labels = labels.reshape(owners, capacity, 1, 2)
    in_q = lax.all_to_all(parcel_q, "dp", split_axis=0, concat_axis=0, tiled=True)
    in_kv = lax.all_to_all(parcel_kv, "dp", split_axis=0, concat_axis=0, tiled=True)
    in_labels = lax.all_to_all(parcel_labels, "dp", split_axis=0, concat_axis=0, tiled=True)
    groups = in_q.shape[2]
    total_rows = in_q.shape[0] * in_q.shape[1]
    targets = in_labels[:, :, 0, 0].reshape(total_rows)
    doc_in = in_labels[:, :, 0, 1].reshape(total_rows)
    local_q = (
        jnp.zeros((rows_dev, groups, group_width), jnp.bfloat16)
        .at[targets]
        .set(in_q.reshape(total_rows, groups, group_width), mode="drop")
    )
    local_kv = (
        jnp.zeros((rows_dev, groups, 2 * head_dim), jnp.bfloat16)
        .at[targets]
        .set(in_kv.reshape(total_rows, groups, 2 * head_dim), mode="drop")
    )
    local_doc = jnp.full((rows_dev,), -1, jnp.int32).at[targets].set(doc_in, mode="drop")
    attended = attend_rows(local_q, local_kv, local_doc)
    return attended.reshape(rows_dev, full_width)


def solution(mesh):
    placed = (
        P(("dp", "ctx"), None),
        P(("dp", "ctx"), None, None, None),
        P(("dp", "ctx"), None),
        P(("dp", "ctx")),
    )
    return jax.shard_map(
        local, mesh=mesh, in_specs=placed, out_specs=P(("dp", "ctx"), None), check_vma=False
    )
```

profile of v0, /device:TPU:25, one launch (start us, length us, event | category | flops | bytes accessed | tf_op | source)
XLA Modules:
  0.0 294.8 jit_solution(11462663096825760531)
XLA Ops:
  8.2 1.9 scatter_fusion
  11.0 11.8 %all-to-all-start = ((s32[32,32,1,2]{1,3,2,0:T(2,128)}), s32[32,32,1,2]{1,3,2,0:T(2,128)S(1)}, u32[]{:S(2)}, u32[]{:S(2)}) async-start(s32[32,32,1,2]{1,3,2,0:T(2,128)} %copy.25), calls=%async_computation | async-start | bytes 65536 | tf_op jit(solution)/shard_map/all_to_all | solution.py:98
  22.7 3.1 %scatter_custom_fusion.2 = bf16[1024,256]{1,0:T(8,128)(2,1)} fusion(s32[512]{0:T(512)S(1)} %bitcast.119, bf16[64,8,2,128]{3,2,1,0:T(2,128)(2,1)S(1)} %bitcast.114, bf16[]{:T(256)} %constant.28.clone.1), kind=kCustom, calls=%fused_computation.39 | custom fusion | bytes 786434 | tf_op jit(solution)/shard_map/scatter | solution.py:83
  25.9 6.5 %all-to-all-done = s32[32,32,1,2]{1,3,2,0:T(2,128)S(1)} async-done(((s32[32,32,1,2]{1,3,2,0:T(2,128)}), s32[32,32,1,2]{1,3,2,0:T(2,128)S(1)}, u32[]{:S(2)}, u32[]{:S(2)}) %all-to-all-start) | async-done | bytes 8224 | tf_op jit(solution)/shard_map/all_to_all | solution.py:98
  32.4 3.9 %all-to-all-start.1 = ((bf16[32,32,1,256]{3,1,2,0:T(8,128)(2,1)}), bf16[32,32,1,256]{3,1,2,0:T(8,128)(2,1)S(1)}, u32[]{:S(2)}, u32[]{:S(2)}) async-start(bf16[32,32,1,256]{3,1,2,0:T(8,128)(2,1)} %bitcast.5), calls=%async_computation.1 | async-start | bytes 1048576 | tf_op jit(solution)/shard_map/all_to_all | solution.py:97
  36.3 4.8 %scatter_custom_fusion.4 = bf16[1024,1024]{1,0:T(8,128)(2,1)} fusion(s32[512]{0:T(512)S(1)} %bitcast.120, bf16[512,1024]{1,0:T(8,128)(2,1)} %param.6, bf16[]{:T(256)} %constant.28.clone.1), kind=kCustom, calls=%fused_computation.35 | custom fusion | bytes 2097664 | tf_op jit(solution)/shard_map/scatter | solution.py:79
  41.2 13.3 %all-to-all-done.1 = bf16[32,32,1,256]{3,1,2,0:T(8,128)(2,1)S(1)} async-done(((bf16[32,32,1,256]{3,1,2,0:T(8,128)(2,1)}), bf16[32,32,1,256]{3,1,2,0:T(8,128)(2,1)S(1)}, u32[]{:S(2)}, u32[]{:S(2)}) %all-to-all-start.1) | async-done | bytes 524320 | tf_op jit(solution)/shard_map/all_to_all | solution.py:97
  54.5 4.9 %all-to-all-start.2 = ((bf16[32,32,1,1024]{3,1,2,0:T(8,128)(2,1)}), bf16[32,32,1,1024]{3,1,2,0:T(8,128)(2,1)S(1)}, u32[]{:S(2)}, u32[]{:S(2)}) async-start(bf16[32,32,1,1024]{3,1,2,0:T(8,128)(2,1)} %bitcast.9), calls=%async_computation.2 | async-start | bytes 4194304 | tf_op jit(solution)/shard_map/all_to_all | solution.py:96
  59.7 5.6 %scatter_custom_fusion.3 = bf16[512,256]{1,0:T(8,128)(2,1)} fusion(s32[1024]{0:T(1024)S(1)} %bitcast.121, bf16[1024,256]{1,0:T(8,128)(2,1)S(1)} %bitcast.113, bf16[]{:T(256)} %constant.28.clone.1), kind=kCustom, calls=%fused_computation.43 | custom fusion | bytes 262146 | tf_op jit(solution)/shard_map/scatter | solution.py:111
  65.4 4.3 %scatter_custom_fusion.1 = s32[512]{0:T(512)S(1)} fusion(s32[1024]{0:T(1024)S(1)} %bitcast.122, s32[1024]{0:T(1024)S(1)} %reshape.186, s32[]{:T(128)} %constant.15.clone.1), kind=kCustom, calls=%fused_computation.53 | custom fusion | bytes 2052 | tf_op jit(solution)/shard_map/scatter | solution.py:113
  69.7 63.0 %all-gather.1 = s32[8,1,512]{2,1,0:T(1,128)S(1)} all-gather(s32[1,1,512]{2,1,0:T(1,128)S(1)} %bitcast.116), channel_id=1, replica_groups=mesh['dp'=32,'ctx'=8] {'ctx'}, dimensions={0}, use_global_device_ids=true | all-gather | bytes 18432 | tf_op jit(solution)/shard_map/all_gather | solution.py:54
  132.8 5.5 %scatter_custom_fusion.5 = bf16[512,1024]{1,0:T(8,128)(2,1)S(1)} fusion(s32[1024]{0:T(1024)S(1)} %bitcast.123, bf16[1024,1024]{1,0:T(8,128)(2,1)S(1)} %bitcast.110, bf16[]{:T(256)} %constant.28.clone.1), kind=kCustom, calls=%fused_computation.37 | custom fusion | bytes 1048578 | tf_op jit(solution)/shard_map/scatter | solution.py:106
  139.5 7.2 %all-gather.4.cloned.1.call-done = bf16[4096,256]{1,0:T(8,128)(2,1)} async-done(((bf16[512,256]{1,0:T(8,128)(2,1)}), bf16[4096,256]{1,0:T(8,128)(2,1)}) %all-gather.4.cloned.1.call-update) | async-done | bytes 2097168 | tf_op jit(solution)/shard_map/all_gather | solution.py:53
  146.6 138.1 %while.15 = (s32[]{:T(128)}, f32[512,1,8]{0,2,1:T(8,128)S(1)}, f32[512,1,8]{0,2,1:T(8,128)S(1)}, f32[512,1,8,128]{0,3,2,1:T(8,128)}, s32[512]{0:T(512)S(1)}, /*i...) while((s32[]{:T(128)}, f32[512,1,8]{0,2,1:T(8,128)S(1)}, ...), condition=%wide.region_9.10_spmd.clone, body=%wide.region_6.9_spmd.clone.sunk | while | flops 1103389696 | bytes 66076856 | solution.py:64
  148.2 1.0 dynamic-slice_bitcast_fusion.2
  149.1 4.7 %fusion.36 = (f32[512,8]{0,1:T(8,128)S(1)}, f32[512,512,8]{1,0,2:T(8,128)}) fusion(pred[512,512]{0,1:T(8,128)(4,1)S(1)} %compare_and_fusion.2, bf16[512,1,8,128]{3,0,2,1:T(8,128)(2,1)S(1)} %get-tuple-element.261, bf16[512,1,256]{2,0,1:T(8,128)(2,1)S(1)} %dynamic-slice_bitcast_fusion.2), kind=kOutput, calls=%fused_computation.9.clone.1 | convolution fusion | flops 543158272 | bytes 9846784 | tf_op jit(solution)/shard_map/while/body/eval_jaxpr/tgqd,kgd->tgqk/dot_general | solution.py:27
  153.9 7.4 %bitcast_add_fusion.5 = f32[512,1,8,128]{0,3,2,1:T(8,128)} fusion(f32[512,1,8,128]{0,3,2,1:T(8,128)} %get-tuple-element.244, f32[512,512,8]{1,0,2:T(8,128)} %get-tuple-element.227, f32[512,8]{0,1:T(8,128)S(1)} %bitcast.106, pred[512,512]{0,1:T(8,128)(4,1)S(1)} %compare_and_fusion.2, f32[512,8]{0,1:T(8,128)S(1)} %get-tuple-element.228, ...), kind=kOutput, calls=%fused_computation.15.clone.1 | convolution fusion | flops 548929536 | bytes 13008897 | tf_op jit(solution)/shard_map/while/body/eval_jaxpr/tgqk,kgd->tgqd/dot_general | solution.py:40
  161.3 2.0 fusion.38
  164.9 1.0 dynamic-slice_bitcast_fusion.2
  165.9 4.7 %fusion.36 = (f32[512,8]{0,1:T(8,128)S(1)}, f32[512,512,8]{1,0,2:T(8,128)}) fusion(pred[512,512]{0,1:T(8,128)(4,1)S(1)} %compare_and_fusion.2, bf16[512,1,8,128]{3,0,2,1:T(8,128)(2,1)S(1)} %get-tuple-element.261, bf16[512,1,256]{2,0,1:T(8,128)(2,1)S(1)} %dynamic-slice_bitcast_fusion.2), kind=kOutput, calls=%fused_computation.9.clone.1 | convolution fusion | flops 543158272 | bytes 9846784 | tf_op jit(solution)/shard_map/while/body/eval_jaxpr/tgqd,kgd->tgqk/dot_general | solution.py:27
  170.6 8.0 %bitcast_add_fusion.5 = f32[512,1,8,128]{0,3,2,1:T(8,128)} fusion(f32[512,1,8,128]{0,3,2,1:T(8,128)} %get-tuple-element.244, f32[512,512,8]{1,0,2:T(8,128)} %get-tuple-element.227, f32[512,8]{0,1:T(8,128)S(1)} %bitcast.106, pred[512,512]{0,1:T(8,128)(4,1)S(1)} %compare_and_fusion.2, f32[512,8]{0,1:T(8,128)S(1)} %get-tuple-element.228, ...), kind=kOutput, calls=%fused_computation.15.clone.1 | convolution fusion | flops 548929536 | bytes 13008897 | tf_op jit(solution)/shard_map/while/body/eval_jaxpr/tgqk,kgd->tgqd/dot_general | solution.py:40
  178.6 2.0 fusion.38
  182.3 1.0 dynamic-slice_bitcast_fusion.2
  183.2 4.7 %fusion.36 = (f32[512,8]{0,1:T(8,128)S(1)}, f32[512,512,8]{1,0,2:T(8,128)}) fusion(pred[512,512]{0,1:T(8,128)(4,1)S(1)} %compare_and_fusion.2, bf16[512,1,8,128]{3,0,2,1:T(8,128)(2,1)S(1)} %get-tuple-element.261, bf16[512,1,256]{2,0,1:T(8,128)(2,1)S(1)} %dynamic-slice_bitcast_fusion.2), kind=kOutput, calls=%fused_computation.9.clone.1 | convolution fusion | flops 543158272 | bytes 9846784 | tf_op jit(solution)/shard_map/while/body/eval_jaxpr/tgqd,kgd->tgqk/dot_general | solution.py:27
  188.0 8.0 %bitcast_add_fusion.5 = f32[512,1,8,128]{0,3,2,1:T(8,128)} fusion(f32[512,1,8,128]{0,3,2,1:T(8,128)} %get-tuple-element.244, f32[512,512,8]{1,0,2:T(8,128)} %get-tuple-element.227, f32[512,8]{0,1:T(8,128)S(1)} %bitcast.106, pred[512,512]{0,1:T(8,128)(4,1)S(1)} %compare_and_fusion.2, f32[512,8]{0,1:T(8,128)S(1)} %get-tuple-element.228, ...), kind=kOutput, calls=%fused_computation.15.clone.1 | convolution fusion | flops 548929536 | bytes 13008897 | tf_op jit(solution)/shard_map/while/body/eval_jaxpr/tgqk,kgd->tgqd/dot_general | solution.py:40
  196.0 2.0 fusion.38
  199.6 1.0 dynamic-slice_bitcast_fusion.2
  200.6 4.7 %fusion.36 = (f32[512,8]{0,1:T(8,128)S(1)}, f32[512,512,8]{1,0,2:T(8,128)}) fusion(pred[512,512]{0,1:T(8,128)(4,1)S(1)} %compare_and_fusion.2, bf16[512,1,8,128]{3,0,2,1:T(8,128)(2,1)S(1)} %get-tuple-element.261, bf16[512,1,256]{2,0,1:T(8,128)(2,1)S(1)} %dynamic-slice_bitcast_fusion.2), kind=kOutput, calls=%fused_computation.9.clone.1 | convolution fusion | flops 543158272 | bytes 9846784 | tf_op jit(solution)/shard_map/while/body/eval_jaxpr/tgqd,kgd->tgqk/dot_general | solution.py:27
  205.3 8.0 %bitcast_add_fusion.5 = f32[512,1,8,128]{0,3,2,1:T(8,128)} fusion(f32[512,1,8,128]{0,3,2,1:T(8,128)} %get-tuple-element.244, f32[512,512,8]{1,0,2:T(8,128)} %get-tuple-element.227, f32[512,8]{0,1:T(8,128)S(1)} %bitcast.106, pred[512,512]{0,1:T(8,128)(4,1)S(1)} %compare_and_fusion.2, f32[512,8]{0,1:T(8,128)S(1)} %get-tuple-element.228, ...), kind=kOutput, calls=%fused_computation.15.clone.1 | convolution fusion | flops 548929536 | bytes 13008897 | tf_op jit(solution)/shard_map/while/body/eval_jaxpr/tgqk,kgd->tgqd/dot_general | solution.py:40
  213.3 2.0 fusion.38
  216.9 1.0 dynamic-slice_bitcast_fusion.2
  217.9 4.7 %fusion.36 = (f32[512,8]{0,1:T(8,128)S(1)}, f32[512,512,8]{1,0,2:T(8,128)}) fusion(pred[512,512]{0,1:T(8,128)(4,1)S(1)} %compare_and_fusion.2, bf16[512,1,8,128]{3,0,2,1:T(8,128)(2,1)S(1)} %get-tuple-element.261, bf16[512,1,256]{2,0,1:T(8,128)(2,1)S(1)} %dynamic-slice_bitcast_fusion.2), kind=kOutput, calls=%fused_computation.9.clone.1 | convolution fusion | flops 543158272 | bytes 9846784 | tf_op jit(solution)/shard_map/while/body/eval_jaxpr/tgqd,kgd->tgqk/dot_general | solution.py:27
  222.6 8.0 %bitcast_add_fusion.5 = f32[512,1,8,128]{0,3,2,1:T(8,128)} fusion(f32[512,1,8,128]{0,3,2,1:T(8,128)} %get-tuple-element.244, f32[512,512,8]{1,0,2:T(8,128)} %get-tuple-element.227, f32[512,8]{0,1:T(8,128)S(1)} %bitcast.106, pred[512,512]{0,1:T(8,128)(4,1)S(1)} %compare_and_fusion.2, f32[512,8]{0,1:T(8,128)S(1)} %get-tuple-element.228, ...), kind=kOutput, calls=%fused_computation.15.clone.1 | convolution fusion | flops 548929536 | bytes 13008897 | tf_op jit(solution)/shard_map/while/body/eval_jaxpr/tgqk,kgd->tgqd/dot_general | solution.py:40
  230.7 2.0 fusion.38
  234.3 1.0 dynamic-slice_bitcast_fusion.2
  235.2 4.7 %fusion.36 = (f32[512,8]{0,1:T(8,128)S(1)}, f32[512,512,8]{1,0,2:T(8,128)}) fusion(pred[512,512]{0,1:T(8,128)(4,1)S(1)} %compare_and_fusion.2, bf16[512,1,8,128]{3,0,2,1:T(8,128)(2,1)S(1)} %get-tuple-element.261, bf16[512,1,256]{2,0,1:T(8,128)(2,1)S(1)} %dynamic-slice_bitcast_fusion.2), kind=kOutput, calls=%fused_computation.9.clone.1 | convolution fusion | flops 543158272 | bytes 9846784 | tf_op jit(solution)/shard_map/while/body/eval_jaxpr/tgqd,kgd->tgqk/dot_general | solution.py:27
  240.0 8.0 %bitcast_add_fusion.5 = f32[512,1,8,128]{0,3,2,1:T(8,128)} fusion(f32[512,1,8,128]{0,3,2,1:T(8,128)} %get-tuple-element.244, f32[512,512,8]{1,0,2:T(8,128)} %get-tuple-element.227, f32[512,8]{0,1:T(8,128)S(1)} %bitcast.106, pred[512,512]{0,1:T(8,128)(4,1)S(1)} %compare_and_fusion.2, f32[512,8]{0,1:T(8,128)S(1)} %get-tuple-element.228, ...), kind=kOutput, calls=%fused_computation.15.clone.1 | convolution fusion | flops 548929536 | bytes 13008897 | tf_op jit(solution)/shard_map/while/body/eval_jaxpr/tgqk,kgd->tgqd/dot_general | solution.py:40
  248.0 2.0 fusion.38
  251.6 1.0 dynamic-slice_bitcast_fusion.2
  252.6 4.7 %fusion.36 = (f32[512,8]{0,1:T(8,128)S(1)}, f32[512,512,8]{1,0,2:T(8,128)}) fusion(pred[512,512]{0,1:T(8,128)(4,1)S(1)} %compare_and_fusion.2, bf16[512,1,8,128]{3,0,2,1:T(8,128)(2,1)S(1)} %get-tuple-element.261, bf16[512,1,256]{2,0,1:T(8,128)(2,1)S(1)} %dynamic-slice_bitcast_fusion.2), kind=kOutput, calls=%fused_computation.9.clone.1 | convolution fusion | flops 543158272 | bytes 9846784 | tf_op jit(solution)/shard_map/while/body/eval_jaxpr/tgqd,kgd->tgqk/dot_general | solution.py:27
  257.3 8.0 %bitcast_add_fusion.5 = f32[512,1,8,128]{0,3,2,1:T(8,128)} fusion(f32[512,1,8,128]{0,3,2,1:T(8,128)} %get-tuple-element.244, f32[512,512,8]{1,0,2:T(8,128)} %get-tuple-element.227, f32[512,8]{0,1:T(8,128)S(1)} %bitcast.106, pred[512,512]{0,1:T(8,128)(4,1)S(1)} %compare_and_fusion.2, f32[512,8]{0,1:T(8,128)S(1)} %get-tuple-element.228, ...), kind=kOutput, calls=%fused_computation.15.clone.1 | convolution fusion | flops 548929536 | bytes 13008897 | tf_op jit(solution)/shard_map/while/body/eval_jaxpr/tgqk,kgd->tgqd/dot_general | solution.py:40
  265.3 2.0 fusion.38
  268.9 1.0 dynamic-slice_bitcast_fusion.2
  269.9 4.7 %fusion.36 = (f32[512,8]{0,1:T(8,128)S(1)}, f32[512,512,8]{1,0,2:T(8,128)}) fusion(pred[512,512]{0,1:T(8,128)(4,1)S(1)} %compare_and_fusion.2, bf16[512,1,8,128]{3,0,2,1:T(8,128)(2,1)S(1)} %get-tuple-element.261, bf16[512,1,256]{2,0,1:T(8,128)(2,1)S(1)} %dynamic-slice_bitcast_fusion.2), kind=kOutput, calls=%fused_computation.9.clone.1 | convolution fusion | flops 543158272 | bytes 9846784 | tf_op jit(solution)/shard_map/while/body/eval_jaxpr/tgqd,kgd->tgqk/dot_general | solution.py:27
  274.7 8.0 %bitcast_add_fusion.5 = f32[512,1,8,128]{0,3,2,1:T(8,128)} fusion(f32[512,1,8,128]{0,3,2,1:T(8,128)} %get-tuple-element.244, f32[512,512,8]{1,0,2:T(8,128)} %get-tuple-element.227, f32[512,8]{0,1:T(8,128)S(1)} %bitcast.106, pred[512,512]{0,1:T(8,128)(4,1)S(1)} %compare_and_fusion.2, f32[512,8]{0,1:T(8,128)S(1)} %get-tuple-element.228, ...), kind=kOutput, calls=%fused_computation.15.clone.1 | convolution fusion | flops 548929536 | bytes 13008897 | tf_op jit(solution)/shard_map/while/body/eval_jaxpr/tgqk,kgd->tgqd/dot_general | solution.py:40
  282.7 2.0 fusion.38
  284.7 1.9 divide_convert_fusion
  286.6 1.3 copy.32
  (94 shorter events, 16.4 us)
Async XLA Ops:
  6.5 1.6 copy-start.1
  8.2 14.6 %copy-start.2 = (bf16[512,1,2,128]{3,2,1,0:T(2,128)(2,1)S(1)}, bf16[512,1,2,128]{3,2,1,0:T(2,128)(2,1)}, u32[]{:S(2)}) copy-start(bf16[512,1,2,128]{3,2,1,0:T(2,128)(2,1)} %param.7) | copy-start | bytes 786436
  11.0 21.4 %all-to-all-start = ((s32[32,32,1,2]{1,3,2,0:T(2,128)}), s32[32,32,1,2]{1,3,2,0:T(2,128)S(1)}, u32[]{:S(2)}, u32[]{:S(2)}) async-start(s32[32,32,1,2]{1,3,2,0:T(2,128)} %copy.25), calls=%async_computation | async-start | bytes 65536 | tf_op jit(solution)/shard_map/all_to_all | solution.py:98
  32.4 22.1 %all-to-all-start.1 = ((bf16[32,32,1,256]{3,1,2,0:T(8,128)(2,1)}), bf16[32,32,1,256]{3,1,2,0:T(8,128)(2,1)S(1)}, u32[]{:S(2)}, u32[]{:S(2)}) async-start(bf16[32,32,1,256]{3,1,2,0:T(8,128)(2,1)} %bitcast.5), calls=%async_computation.1 | async-start | bytes 1048576 | tf_op jit(solution)/shard_map/all_to_all | solution.py:97
  54.5 78.3 %all-to-all-start.2 = ((bf16[32,32,1,1024]{3,1,2,0:T(8,128)(2,1)}), bf16[32,32,1,1024]{3,1,2,0:T(8,128)(2,1)S(1)}, u32[]{:S(2)}, u32[]{:S(2)}) async-start(bf16[32,32,1,1024]{3,1,2,0:T(8,128)(2,1)} %bitcast.9), calls=%async_computation.2 | async-start | bytes 4194304 | tf_op jit(solution)/shard_map/all_to_all | solution.py:96
  59.4 87.2 %all-gather.4.cloned.1.call-start = ((), (), s32[]{:S(2)}) async-start(), calls=%async_computation.3 | async-start | bytes 2359296 | tf_op jit(solution)/shard_map/all_gather | solution.py:53
  153.9 7.4 %copy-start = (f32[512,512,8]{1,0,2:T(8,128)S(1)}, f32[512,512,8]{1,0,2:T(8,128)}, u32[]{:S(2)}) copy-start(f32[512,512,8]{1,0,2:T(8,128)} %get-tuple-element.227) | copy-start | bytes 25165828 | tf_op jit(solution)/shard_map/while
  170.6 8.0 %copy-start = (f32[512,512,8]{1,0,2:T(8,128)S(1)}, f32[512,512,8]{1,0,2:T(8,128)}, u32[]{:S(2)}) copy-start(f32[512,512,8]{1,0,2:T(8,128)} %get-tuple-element.227) | copy-start | bytes 25165828 | tf_op jit(solution)/shard_map/while
  187.9 8.0 %copy-start = (f32[512,512,8]{1,0,2:T(8,128)S(1)}, f32[512,512,8]{1,0,2:T(8,128)}, u32[]{:S(2)}) copy-start(f32[512,512,8]{1,0,2:T(8,128)} %get-tuple-element.227) | copy-start | bytes 25165828 | tf_op jit(solution)/shard_map/while
  205.3 8.0 %copy-start = (f32[512,512,8]{1,0,2:T(8,128)S(1)}, f32[512,512,8]{1,0,2:T(8,128)}, u32[]{:S(2)}) copy-start(f32[512,512,8]{1,0,2:T(8,128)} %get-tuple-element.227) | copy-start | bytes 25165828 | tf_op jit(solution)/shard_map/while
  222.6 8.0 %copy-start = (f32[512,512,8]{1,0,2:T(8,128)S(1)}, f32[512,512,8]{1,0,2:T(8,128)}, u32[]{:S(2)}) copy-start(f32[512,512,8]{1,0,2:T(8,128)} %get-tuple-element.227) | copy-start | bytes 25165828 | tf_op jit(solution)/shard_map/while
  240.0 8.0 %copy-start = (f32[512,512,8]{1,0,2:T(8,128)S(1)}, f32[512,512,8]{1,0,2:T(8,128)}, u32[]{:S(2)}) copy-start(f32[512,512,8]{1,0,2:T(8,128)} %get-tuple-element.227) | copy-start | bytes 25165828 | tf_op jit(solution)/shard_map/while
  257.3 8.0 %copy-start = (f32[512,512,8]{1,0,2:T(8,128)S(1)}, f32[512,512,8]{1,0,2:T(8,128)}, u32[]{:S(2)}) copy-start(f32[512,512,8]{1,0,2:T(8,128)} %get-tuple-element.227) | copy-start | bytes 25165828 | tf_op jit(solution)/shard_map/while
  274.6 8.0 %copy-start = (f32[512,512,8]{1,0,2:T(8,128)S(1)}, f32[512,512,8]{1,0,2:T(8,128)}, u32[]{:S(2)}) copy-start(f32[512,512,8]{1,0,2:T(8,128)} %get-tuple-element.227) | copy-start | bytes 25165828 | tf_op jit(solution)/shard_map/while
Sparse Core Ops, SparseCore 0:
  65.4 81.1 all-gather.3
where the time goes:
time: 298 us; the launch traced here: 295 us
  matrix products  101 us (34%)
  blocking collectives  63 us (21%)
  local copies, waits for them, and re-layouts  41.6 us (14%)
  other arithmetic  27.1 us (9%)
  waiting for transfers between devices  27 us (9%)
  starting transfers between devices  20.7 us (7%)
  between operations  13.6 us (5%)
    dot_general x8, matrix products, update(): jnp.einsum('tgqk,kgd->tgqd', weights.astype(jnp.bfloat16), block_kv[:, :,...  63.5 us
    all_gather x1, blocking collectives, attend_rows(): block_doc = lax.all_gather(local_doc, 'ctx', axis=0, tiled=True)  63 us
    dot_general x8, matrix products, update(): jnp.einsum('tgqd,kgd->tgqk', query_heads, block_kv[:, :, :head_dim], pref...  37.6 us
    reduce_sum x8, other arithmetic, update(): new_totals = totals * decay + jnp.sum(weights, axis=-1)  16.1 us
    all_to_all x1, waiting for transfers between devices, local(): lax.all_to_all(parcel_kv, 'dp', split_axis=0, concat_axis=0, tiled=True)  13.3 us
    all_to_all x1, starting transfers between devices, local(): lax.all_to_all(parcel_labels, 'dp', split_axis=0, concat_axis=0, tiled=True)  11.8 us
    squeeze x8, local copies, waits for them, and re-layouts, attend_rows(): state_out, unused = lax.scan(step, initial, (split_kv, split_doc, offsets))  7.79 us
    all_gather x1, waiting for transfers between devices, attend_rows(): block_kv = lax.all_gather(local_kv, 'ctx', axis=0, tiled=True)  7.16 us
  transfers between devices with their start and end apart: 4, of which 3 were waited for; matrix products, arithmetic and copies ran while one was open for 8% of the time, Pallas kernels for 0%

commit v1 on v0

v1 whole, which is shorter than its diff:
```python
import functools
import math

import jax
import jax.numpy as jnp
from jax import lax
from jax.experimental import pallas as pl
from jax.experimental.pallas import tpu as pltpu
from jax.sharding import PartitionSpec as P

MESH = pl.DeviceIdType.MESH
F32, BF16, I32 = jnp.float32, jnp.bfloat16, jnp.int32
DP, CTX = 32, 8
ROWS, HEADS, HD, CAP = 512, 8, 128, 32
BLOCKS = ROWS // CAP
PER = 2
CHUNKS = HEADS // PER
WIDE = PER * HD
TALL = PER * ROWS
SEQ = 4096
NEG = -1e30
FACTOR = math.log2(math.e) / math.sqrt(HD)


def kernel(
    key, labs, q_hbm, kv_hbm, out_hbm,
    q_v, kv_v, lab_s, lab_r, kv_s, kv_r, q_s, q_r,
    spread, gather, begin, k_all, v_all, q_two, scores, out_v,
    in_sem, lab_ss, lab_rs, kv_ss, kv_rs, q_ss, q_rs,
    k_ss, v_ss, k_rs, v_rs, out_sem,
):
    me, cx = lax.axis_index("dp"), lax.axis_index("ctx")
    y, low = cx // 2, cx % 2
    mate = y * 2 + (1 - low)

    barrier = pltpu.get_barrier_semaphore()

    def greet(j, _):
        pl.semaphore_signal(
            barrier, inc=1, device_id=((me + j) % DP, cx), device_id_type=MESH
        )
        return 0

    lax.fori_loop(1, DP, greet, 0)
    pl.semaphore_signal(barrier, inc=1, device_id=(me, mate), device_id_type=MESH)
    for dy in (1, 2, 3):
        pl.semaphore_signal(
            barrier, inc=1, device_id=(me, (y + dy) % 4 * 2 + low), device_id_type=MESH
        )

    get_kv = pltpu.make_async_copy(kv_hbm, kv_v, in_sem.at[0])
    get_q = pltpu.make_async_copy(q_hbm, q_v, in_sem.at[1])
    get_kv.start()
    get_q.start()
    lab_s[...] = labs[...]
    get_kv.wait()

    slots = DP * CAP
    spread[...] = jnp.where(
        key[...] == lax.broadcasted_iota(I32, (slots, ROWS), 0), 1.0, 0.0
    ).astype(BF16)

    def packed(x):
        part = jnp.dot(spread[...], x, preferred_element_type=F32)
        return part.astype(BF16).reshape(DP, CAP, x.shape[1])

    kv_s[...] = packed(kv_v[...])
    pl.semaphore_wait(barrier, DP - 1 + 4)

    def send_kv(j, _):
        there = ((me + j) % DP, cx)
        pltpu.make_async_remote_copy(
            lab_s.at[j], lab_r.at[j], lab_ss, lab_rs, device_id=there, device_id_type=MESH
        ).start()
        pltpu.make_async_remote_copy(
            kv_s.at[j], kv_r.at[j], kv_ss, kv_rs, device_id=there, device_id_type=MESH
        ).start()
        return 0

    lax.fori_loop(1, DP, send_kv, 0)
    lab_r[0] = lab_s[0]
    kv_r[0] = kv_s[0]
    get_q.wait()

    for ch in range(CHUNKS):

        q_s[ch] = packed(q_v[:, ch * WIDE : (ch + 1) * WIDE])

        def send_q(j, _):
            pltpu.make_async_remote_copy(
                q_s.at[ch, j], q_r.at[ch, j], q_ss.at[ch], q_rs.at[ch],
                device_id=((me + j) % DP, cx), device_id_type=MESH,
            ).start()
            return 0

        lax.fori_loop(1, DP, send_q, 0)
        q_r[ch, 0] = q_s[ch, 0]

    others = pl.ds(1, DP - 1)

    def group(src, dst, send, recv):
        return pltpu.make_async_remote_copy(
            src, dst, send, recv, device_id=((me + 1) % DP, cx), device_id_type=MESH
        )

    labels = group(lab_s.at[others], lab_r.at[others], lab_ss, lab_rs)
    labels.wait_recv()
    lab = lab_r[:, 0, :]
    lane = lax.broadcasted_iota(I32, (DP, HD), 1)
    place = jnp.sum(jnp.where(lane == CAP, lab, 0), axis=1, keepdims=True)
    slot = lax.broadcasted_iota(I32, (DP, HD), 0)
    place_row = jnp.sum(jnp.where(slot == lane, place, 0), axis=0, keepdims=True)
    block_row = lax.broadcasted_iota(I32, (ROWS, HD), 0) // CAP
    owner = jnp.where(place_row == block_row + 1, 1.0, 0.0).astype(BF16)
    widen = jnp.where(
        lax.broadcasted_iota(I32, (HD, slots), 1) // CAP
        == lax.broadcasted_iota(I32, (HD, slots), 0),
        1.0,
        0.0,
    ).astype(BF16)
    same = (
        lax.broadcasted_iota(I32, (ROWS, slots), 0) % CAP
        == lax.broadcasted_iota(I32, (ROWS, slots), 1) % CAP
    )
    gather[...] = jnp.where(
        same, jnp.dot(owner, widen, preferred_element_type=F32), 0.0
    ).astype(BF16)
    square = lax.broadcasted_iota(I32, (CAP, HD), 0) == lax.broadcasted_iota(I32, (CAP, HD), 1)
    for b in range(BLOCKS):
        row = jnp.sum(jnp.where(place == b + 1, lab, 0), axis=0, keepdims=True)
        column = jnp.sum(jnp.where(square, row, 0), axis=1, keepdims=True)
        begin[b * CAP : (b + 1) * CAP, :] = jnp.broadcast_to(column, (CAP, HD))

    def unpacked(x):
        return jnp.dot(gather[...], x.reshape(slots, x.shape[2]), preferred_element_type=F32)

    group(kv_s.at[others], kv_r.at[others], kv_ss, kv_rs).wait_recv()
    own = unpacked(kv_r[...])
    v_all[cx] = own[:, HD:].astype(BF16)
    k_all[cx] = jnp.transpose(own[:, :HD]).astype(BF16)

    def ctx_copies(n, block, there):
        return [
            pltpu.make_async_remote_copy(
                a.at[block], a.at[block], s.at[n], r.at[block],
                device_id=(me, there), device_id_type=MESH,
            )
            for a, s, r in ((k_all, k_ss, k_rs), (v_all, v_ss, v_rs))
        ]

    to_mate = (low == 0) | (y < 3)
    ups = [(dy, y + dy < 4, (y + dy) % 4 * 2 + low) for dy in (1, 2, 3)]

    @pl.when(to_mate)
    def _():
        for c in ctx_copies(0, cx, mate):
            c.start()

    for dy, live, there in ups:

        @pl.when(live)
        def _(dy=dy, there=there):
            for c in ctx_copies(dy, cx, there):
                c.start()

    @pl.when((low == 1) | (y < 3))
    def _():
        for c in ctx_copies(0, mate, mate):
            c.wait_recv()

    for dy, live, there in ups:

        @pl.when(live)
        def _(dy=dy, there=there):
            for c in ctx_copies(3 + dy, mate, there):
                c.start()

    ones = jnp.ones((ROWS, HD), BF16)
    key_lane = lax.broadcasted_iota(I32, (ROWS, ROWS), 1)
    key_sub = lax.broadcasted_iota(I32, (ROWS, ROWS), 0)

    def score(kb, diagonal):
        kt = k_all[kb]
        s = jnp.dot(
            q_two[...], jnp.concatenate([kt, kt], axis=0), preferred_element_type=F32
        )
        first = jnp.concatenate([begin[...]] * (ROWS // HD), axis=1)
        keep = key_lane + kb * ROWS >= first
        if diagonal:
            keep = keep & (key_lane <= key_sub)
        parts = [
            jnp.where(keep, s[h * ROWS : (h + 1) * ROWS], NEG) for h in range(PER)
        ]
        return jnp.concatenate(parts, axis=0)

    def widest(top, s):
        for i in range(ROWS // HD):
            top = jnp.maximum(top, s[:, i * HD : (i + 1) * HD])
        return top

    def chunk(ch, _):
        group(
            q_s.at[ch, others], q_r.at[ch, others], q_ss.at[ch], q_rs.at[ch]
        ).wait_recv()
        mine = unpacked(q_r[ch]) * FACTOR
        high = mine.astype(BF16)
        rest = (mine - high.astype(F32)).astype(BF16)
        for h in range(PER):
            at, cols = slice(h * ROWS, (h + 1) * ROWS), slice(h * HD, (h + 1) * HD)
            q_two[at, :HD] = high[:, cols]
            q_two[at, HD:] = rest[:, cols]
        s = score(cx, True)
        scores[0] = s
        top = widest(jnp.full((TALL, HD), NEG, F32), s)

        def first_pass(i, top):
            kb = cx - i

            @pl.when((ch == 0) & (kb // 2 < y))
            def _():
                for c in ctx_copies(0, kb, mate):
                    c.wait_recv()

            s = score(kb, False)
            scores[i] = s
            return widest(top, s)

        top = lax.fori_loop(1, cx + 1, first_pass, top)
        peak = jnp.max(top, axis=1, keepdims=True)

        def second_pass(i, total):
            w = jnp.exp2(scores[i] - peak).astype(BF16)
            v = jnp.concatenate([v_all[cx - i], ones], axis=1)
            return total + jnp.dot(w, v, preferred_element_type=F32)

        total = lax.fori_loop(0, cx + 1, second_pass, jnp.zeros((TALL, 2 * HD), F32))
        done = (total[:, :HD] / total[:, HD:]).astype(BF16)
        for h in range(PER):
            out_v[ch, :, h * HD : (h + 1) * HD] = done[h * ROWS : (h + 1) * ROWS]
        put(ch).start()
        return 0

    def put(ch):
        at = pl.ds(pl.multiple_of(ch * WIDE, WIDE), WIDE)
        return pltpu.make_async_copy(out_v.at[ch], out_hbm.at[:, at], out_sem.at[ch])

    lax.fori_loop(0, CHUNKS, chunk, 0)

    labels.wait_send()
    group(kv_s.at[others], kv_r.at[others], kv_ss, kv_rs).wait_send()
    for ch in range(CHUNKS):
        group(
            q_s.at[ch, others], q_r.at[ch, others], q_ss.at[ch], q_rs.at[ch]
        ).wait_send()

    @pl.when(to_mate)
    def _():
        for c in ctx_copies(0, cx, mate):
            c.wait_send()

    for dy, live, there in ups:

        @pl.when(live)
        def _(dy=dy, there=there):
            for c in ctx_copies(dy, cx, there):
                c.wait_send()
            for c in ctx_copies(3 + dy, mate, there):
                c.wait_send()

    for ch in range(CHUNKS):
        put(ch).wait()


def local(queries, keys_values, routing, documents):
    me = lax.axis_index("dp")
    head = routing.reshape(BLOCKS, CAP, 2)[:, 0, :]
    turn = (head[:, 0] - me) % DP
    hit = turn[None, :] == jnp.arange(DP, dtype=I32)[:, None]
    turns = (routing[:, 0] - me) % DP * CAP + jnp.arange(ROWS, dtype=I32) % CAP
    notes = jnp.concatenate(
        [documents.reshape(BLOCKS, CAP) % SEQ, head[:, 1:] // CAP + 1], axis=1
    )
    notes = jnp.pad(notes, ((0, 0), (0, HD - CAP - 1)))
    labs = jnp.sum(jnp.where(hit[:, :, None], notes[None], 0), axis=1)
    dma = pltpu.SemaphoreType.DMA
    vmem, anywhere = pl.BlockSpec(memory_space=pltpu.VMEM), pl.BlockSpec(memory_space=pl.ANY)
    return pl.pallas_call(
        kernel,
        out_shape=jax.ShapeDtypeStruct((ROWS, HEADS * HD), BF16),
        in_specs=[vmem, vmem, anywhere, anywhere],
        out_specs=anywhere,
        scratch_shapes=[
            pltpu.VMEM((ROWS, HEADS * HD), BF16),
            pltpu.VMEM((ROWS, 2 * HD), BF16),
            pltpu.VMEM((DP, 1, HD), I32),
            pltpu.VMEM((DP, 1, HD), I32),
            pltpu.VMEM((DP, CAP, 2 * HD), BF16),
            pltpu.VMEM((DP, CAP, 2 * HD), BF16),
            pltpu.VMEM((CHUNKS, DP, CAP, WIDE), BF16),
            pltpu.VMEM((CHUNKS, DP, CAP, WIDE), BF16),
            pltpu.VMEM((DP * CAP, ROWS), BF16),
            pltpu.VMEM((ROWS, DP * CAP), BF16),
            pltpu.VMEM((ROWS, HD), I32),
            pltpu.VMEM((CTX, HD, ROWS), BF16),
            pltpu.VMEM((CTX, ROWS, HD), BF16),
            pltpu.VMEM((TALL, 2 * HD), BF16),
            pltpu.VMEM((CTX, TALL, ROWS), F32),
            pltpu.VMEM((CHUNKS, ROWS, WIDE), BF16),
            dma((2,)), dma, dma, dma, dma, dma((CHUNKS,)), dma((CHUNKS,)),
            dma((7,)), dma((7,)), dma((CTX,)), dma((CTX,)), dma((CHUNKS,)),
        ],
        compiler_params=pltpu.CompilerParams(
            collective_id=1, has_side_effects=True, vmem_limit_bytes=56 << 20
        ),
        cost_estimate=pl.CostEstimate(
            flops=8 << 30, bytes_accessed=4 << 20, transcendentals=16 << 20
        ),
        name="relay_attend",
    )(turns.reshape(1, ROWS), labs.reshape(DP, 1, HD), queries, keys_values.reshape(ROWS, 2 * HD))


def solution(mesh):
    placed = (
        P(("dp", "ctx"), None),
        P(("dp", "ctx"), None, None, None),
        P(("dp", "ctx"), None),
        P(("dp", "ctx")),
    )
    return jax.shard_map(
        local, mesh=mesh, in_specs=placed, out_specs=P(("dp", "ctx"), None), check_vma=False
    )
```

time: 298 us -> 129 us (0.43)
  the two profiles are of different devices: /device:TPU:25 before, /device:TPU:56 now
where the time goes in v1:
time: 129 us; the launch traced here: 128 us
  Pallas kernels  122 us (95%)
  local copies, waits for them, and re-layouts  5.05 us (4%)
  other arithmetic  1.48 us (1%)
    pallas_call x1, Pallas kernels, local(): pl.pallas_call(kernel, out_shape=jax.ShapeDtypeStruct((ROWS, HEADS * HD),...  122 us
    unnamed x7, local copies, waits for them, and re-layouts  4.8 us

profile of v1, /device:TPU:56, one launch (start us, length us, event | category | flops | bytes accessed | tf_op | source)
XLA Modules:
  0.0 128.4 jit_solution(18356758781665126616)
XLA Ops:
  0.0 0.0 copy-start
  0.0 0.7 copy-done
  0.7 0.0 copy-start.1
  0.7 0.6 fusion.1.key
  1.3 0.1 copy-done.1
  1.4 0.1 reshape.125
  1.5 0.1 reshape.124
  1.5 0.1 copy.9
  1.7 0.1 copy.8
  1.8 0.1 pad_add_fusion
  1.8 0.8 select_reduce_fusion
  2.6 1.7 %copy.12 = bf16[64,8,2,128]{3,1,2,0:T(8,128)(2,1)} copy(bf16[64,8,2,128]{3,2,1,0:T(2,128)(2,1)} %bitcast.14) | data formatting | bytes 524288
  4.3 121.8 %relay_attend.1 = bf16[512,1024]{1,0:T(8,128)(2,1)} custom-call(s32[1,512]{1,0:T(1,128)} %fusion.1.key, s32[32,1,128]{2,1,0:T(1,128)} %bitcast.17, bf16[512,1024]{1,0:T(8,128)(2,1)} %q_hbm.1, bf16[512,256]{1,0:T(8,128)(2,1)} %bitcast.15), custom_call_target="tpu_custom_call" | custom-call | flops 8589934592 | bytes 4194304 | tf_op jit(solution)/shard_map/relay_attend/pallas_call | solution.py:287
  126.1 2.3 %copy.14 = bf16[512,1024]{1,0:T(8,128)(2,1)} copy(bf16[512,1024]{1,0:T(8,128)(2,1)} %relay_attend.1) | data formatting | bytes 2097152
  (5 shorter events, 0.1 us)
Async XLA Ops:
  0.0 0.7 copy-start
  0.7 0.7 copy-start.1

commit v2 on v1

--- a/solution.py
+++ b/solution.py
@@ -17,14 +17,15 @@
 CHUNKS = HEADS // PER
 WIDE = PER * HD
 TALL = PER * ROWS
+PAIR = 2 * ROWS
 SEQ = 4096
 NEG = -1e30
 FACTOR = math.log2(math.e) / math.sqrt(HD)
 
 
 def kernel(
-    key, labs, q_hbm, kv_hbm, out_hbm,
-    q_v, kv_v, lab_s, lab_r, kv_s, kv_r, q_s, q_r,
+    route_hbm, doc_hbm, q_hbm, kv_hbm, out_hbm,
+    route_v, doc_v, q_v, kv_v, lab_s, lab_r, kv_s, kv_r, q_s, q_r,
     spread, gather, begin, k_all, v_all, q_two, scores, out_v,
     in_sem, lab_ss, lab_rs, kv_ss, kv_rs, q_ss, q_rs,
     k_ss, v_ss, k_rs, v_rs, out_sem,
@@ -48,23 +49,38 @@
             barrier, inc=1, device_id=(me, (y + dy) % 4 * 2 + low), device_id_type=MESH
         )
 
-    get_kv = pltpu.make_async_copy(kv_hbm, kv_v, in_sem.at[0])
-    get_q = pltpu.make_async_copy(q_hbm, q_v, in_sem.at[1])
-    get_kv.start()
-    get_q.start()
-    lab_s[...] = labs[...]
-    get_kv.wait()
-
+    gets = [
+        pltpu.make_async_copy(a, b, in_sem.at[n])
+        for n, (a, b) in enumerate(
+            ((route_hbm, route_v), (doc_hbm, doc_v), (kv_hbm, kv_v), (q_hbm, q_v))
+        )
+    ]
+    for get in gets:
+        get.start()
+    for get in gets[:2]:
+        get.wait()
+    turn = (route_v[0:1, :] - me) & (DP - 1)
+    note = (doc_v[...] & (SEQ - 1)) * CAP + route_v[1:2, :] // CAP + 1
+    key = turn * CAP + (lax.broadcasted_iota(I32, (1, ROWS), 1) & (CAP - 1))
     slots = DP * CAP
     spread[...] = jnp.where(
-        key[...] == lax.broadcasted_iota(I32, (slots, ROWS), 0), 1.0, 0.0
+        key == lax.broadcasted_iota(I32, (slots, ROWS), 0), 1.0, 0.0
     ).astype(BF16)
+    slot = lax.broadcasted_iota(I32, (DP, HD), 0)
+    lane = lax.broadcasted_iota(I32, (DP, HD), 1)
+    labs = jnp.zeros((DP, HD), I32)
+    for i in range(ROWS // HD):
+        part = slice(i * HD, (i + 1) * HD)
+        labs = labs + jnp.where(turn[:, part] == slot, note[:, part], 0)
+    for j in range(DP):
+        lab_s[j] = labs[j : j + 1]
+    gets[2].wait()
 
     def packed(x):
         part = jnp.dot(spread[...], x, preferred_element_type=F32)
         return part.astype(BF16).reshape(DP, CAP, x.shape[1])
 
-    kv_s[...] = packed(kv_v[...])
+    kv_s[...] = packed(jnp.concatenate([kv_v[:, 0, :], kv_v[:, 1, :]], axis=1))
     pl.semaphore_wait(barrier, DP - 1 + 4)
 
     def send_kv(j, _):
@@ -80,12 +96,13 @@
     lax.fori_loop(1, DP, send_kv, 0)
     lab_r[0] = lab_s[0]
     kv_r[0] = kv_s[0]
-    get_q.wait()
-
-    for ch in range(CHUNKS):
-
+    gets[3].wait()
+
+    def pack_q(ch):
         q_s[ch] = packed(q_v[:, ch * WIDE : (ch + 1) * WIDE])
-
+        q_r[ch, 0] = q_s[ch, 0]
+
+    def send_chunk(ch):
         def send_q(j, _):
             pltpu.make_async_remote_copy(
                 q_s.at[ch, j], q_r.at[ch, j], q_ss.at[ch], q_rs.at[ch],
@@ -94,8 +111,11 @@
             return 0
 
         lax.fori_loop(1, DP, send_q, 0)
-        q_r[ch, 0] = q_s[ch, 0]
-
+
+    pack_q(0)
+    send_chunk(0)
+    for ch in range(1, CHUNKS):
+        pack_q(ch)
     others = pl.ds(1, DP - 1)
 
     def group(src, dst, send, recv):
@@ -106,9 +126,7 @@
     labels = group(lab_s.at[others], lab_r.at[others], lab_ss, lab_rs)
     labels.wait_recv()
     lab = lab_r[:, 0, :]
-    lane = lax.broadcasted_iota(I32, (DP, HD), 1)
-    place = jnp.sum(jnp.where(lane == CAP, lab, 0), axis=1, keepdims=True)
-    slot = lax.broadcasted_iota(I32, (DP, HD), 0)
+    place = jnp.max(lab & (CAP - 1), axis=1, keepdims=True)
     place_row = jnp.sum(jnp.where(slot == lane, place, 0), axis=0, keepdims=True)
     block_row = lax.broadcasted_iota(I32, (ROWS, HD), 0) // CAP
     owner = jnp.where(place_row == block_row + 1, 1.0, 0.0).astype(BF16)
@@ -125,9 +143,11 @@
     gather[...] = jnp.where(
         same, jnp.dot(owner, widen, preferred_element_type=F32), 0.0
     ).astype(BF16)
-    square = lax.broadcasted_iota(I32, (CAP, HD), 0) == lax.broadcasted_iota(I32, (CAP, HD), 1)
+    square = (lax.broadcasted_iota(I32, (CAP, HD), 1) & (CAP - 1)) == lax.broadcasted_iota(
+        I32, (CAP, HD), 0
+    )
     for b in range(BLOCKS):
-        row = jnp.sum(jnp.where(place == b + 1, lab, 0), axis=0, keepdims=True)
+        row = jnp.sum(jnp.where(place == b + 1, lab // CAP, 0), axis=0, keepdims=True)
         column = jnp.sum(jnp.where(square, row, 0), axis=1, keepdims=True)
         begin[b * CAP : (b + 1) * CAP, :] = jnp.broadcast_to(column, (CAP, HD))
 
@@ -148,13 +168,10 @@
             for a, s, r in ((k_all, k_ss, k_rs), (v_all, v_ss, v_rs))
         ]
 
-    to_mate = (low == 0) | (y < 3)
     ups = [(dy, y + dy < 4, (y + dy) % 4 * 2 + low) for dy in (1, 2, 3)]
 
-    @pl.when(to_mate)
-    def _():
-        for c in ctx_copies(0, cx, mate):
-            c.start()
+    for c in ctx_copies(0, cx, mate):
+        c.start()
 
     for dy, live, there in ups:
 
@@ -163,10 +180,9 @@
             for c in ctx_copies(dy, cx, there):
                 c.start()
 
-    @pl.when((low == 1) | (y < 3))
-    def _():
-        for c in ctx_copies(0, mate, mate):
-            c.wait_recv()
+    send_chunk(1)
+    for c in ctx_copies(0, mate, mate):
+        c.wait_recv()
 
     for dy, live, there in ups:
 
@@ -175,26 +191,28 @@
             for c in ctx_copies(3 + dy, mate, there):
                 c.start()
 
-    ones = jnp.ones((ROWS, HD), BF16)
-    key_lane = lax.broadcasted_iota(I32, (ROWS, ROWS), 1)
-    key_sub = lax.broadcasted_iota(I32, (ROWS, ROWS), 0)
-
-    def score(kb, diagonal):
-        kt = k_all[kb]
+    send_chunk(2)
+    send_chunk(3)
+    ones = jnp.ones((PAIR, HD), BF16)
+    key_lane = lax.broadcasted_iota(I32, (ROWS, PAIR), 1)
+    query_row = lax.broadcasted_iota(I32, (ROWS, PAIR), 0) + low * ROWS
+
+    def score(pair, diagonal):
+        kt = jnp.concatenate([k_all[2 * pair], k_all[2 * pair + 1]], axis=1)
         s = jnp.dot(
             q_two[...], jnp.concatenate([kt, kt], axis=0), preferred_element_type=F32
         )
-        first = jnp.concatenate([begin[...]] * (ROWS // HD), axis=1)
-        keep = key_lane + kb * ROWS >= first
+        first = jnp.concatenate([begin[...]] * (PAIR // HD), axis=1)
+        keep = key_lane + pair * PAIR >= first
         if diagonal:
-            keep = keep & (key_lane <= key_sub)
+            keep = keep & (key_lane <= query_row)
         parts = [
             jnp.where(keep, s[h * ROWS : (h + 1) * ROWS], NEG) for h in range(PER)
         ]
         return jnp.concatenate(parts, axis=0)
 
     def widest(top, s):
-        for i in range(ROWS // HD):
+        for i in range(PAIR // HD):
             top = jnp.maximum(top, s[:, i * HD : (i + 1) * HD])
         return top
 
@@ -209,31 +227,34 @@
             at, cols = slice(h * ROWS, (h + 1) * ROWS), slice(h * HD, (h + 1) * HD)
             q_two[at, :HD] = high[:, cols]
             q_two[at, HD:] = rest[:, cols]
-        s = score(cx, True)
+        s = score(y, True)
         scores[0] = s
         top = widest(jnp.full((TALL, HD), NEG, F32), s)
 
         def first_pass(i, top):
-            kb = cx - i
-
-            @pl.when((ch == 0) & (kb // 2 < y))
+            pair = y - i
+
+            @pl.when(ch == 0)
             def _():
-                for c in ctx_copies(0, kb, mate):
-                    c.wait_recv()
-
-            s = score(kb, False)
+                for block in (2 * pair, 2 * pair + 1):
+                    for c in ctx_copies(0, block, mate):
+                        c.wait_recv()
+
+            s = score(pair, False)
             scores[i] = s
             return widest(top, s)
 
-        top = lax.fori_loop(1, cx + 1, first_pass, top)
+        top = lax.fori_loop(1, y + 1, first_pass, top)
         peak = jnp.max(top, axis=1, keepdims=True)
 
         def second_pass(i, total):
             w = jnp.exp2(scores[i] - peak).astype(BF16)
-            v = jnp.concatenate([v_all[cx - i], ones], axis=1)
+            pair = y - i
+            v = jnp.concatenate([v_all[2 * pair], v_all[2 * pair + 1]], axis=0)
+            v = jnp.concatenate([v, ones], axis=1)
             return total + jnp.dot(w, v, preferred_element_type=F32)
 
-        total = lax.fori_loop(0, cx + 1, second_pass, jnp.zeros((TALL, 2 * HD), F32))
+        total = lax.fori_loop(0, y + 1, second_pass, jnp.zeros((TALL, 2 * HD), F32))
         done = (total[:, :HD] / total[:, HD:]).astype(BF16)
         for h in range(PER):
             out_v[ch, :, h * HD : (h + 1) * HD] = done[h * ROWS : (h + 1) * ROWS]
@@ -253,10 +274,8 @@
             q_s.at[ch, others], q_r.at[ch, others], q_ss.at[ch], q_rs.at[ch]
         ).wait_send()
 
-    @pl.when(to_mate)
-    def _():
-        for c in ctx_copies(0, cx, mate):
-            c.wait_send()
+    for c in ctx_copies(0, cx, mate):
+        c.wait_send()
 
     for dy, live, there in ups:
 
@@ -272,26 +291,18 @@
 
 
 def local(queries, keys_values, routing, documents):
-    me = lax.axis_index("dp")
-    head = routing.reshape(BLOCKS, CAP, 2)[:, 0, :]
-    turn = (head[:, 0] - me) % DP
-    hit = turn[None, :] == jnp.arange(DP, dtype=I32)[:, None]
-    turns = (routing[:, 0] - me) % DP * CAP + jnp.arange(ROWS, dtype=I32) % CAP
-    notes = jnp.concatenate(
-        [documents.reshape(BLOCKS, CAP) % SEQ, head[:, 1:] // CAP + 1], axis=1
-    )
-    notes = jnp.pad(notes, ((0, 0), (0, HD - CAP - 1)))
-    labs = jnp.sum(jnp.where(hit[:, :, None], notes[None], 0), axis=1)
     dma = pltpu.SemaphoreType.DMA
-    vmem, anywhere = pl.BlockSpec(memory_space=pltpu.VMEM), pl.BlockSpec(memory_space=pl.ANY)
+    anywhere = pl.BlockSpec(memory_space=pl.ANY)
     return pl.pallas_call(
         kernel,
         out_shape=jax.ShapeDtypeStruct((ROWS, HEADS * HD), BF16),
-        in_specs=[vmem, vmem, anywhere, anywhere],
+        in_specs=[anywhere] * 4,
         out_specs=anywhere,
         scratch_shapes=[
+            pltpu.VMEM((2, ROWS), I32),
+            pltpu.VMEM((1, ROWS), I32),
             pltpu.VMEM((ROWS, HEADS * HD), BF16),
-            pltpu.VMEM((ROWS, 2 * HD), BF16),
+            pltpu.VMEM((ROWS, 2, HD), BF16),
             pltpu.VMEM((DP, 1, HD), I32),
             pltpu.VMEM((DP, 1, HD), I32),
             pltpu.VMEM((DP, CAP, 2 * HD), BF16),
@@ -304,9 +315,9 @@
             pltpu.VMEM((CTX, HD, ROWS), BF16),
             pltpu.VMEM((CTX, ROWS, HD), BF16),
             pltpu.VMEM((TALL, 2 * HD), BF16),
-            pltpu.VMEM((CTX, TALL, ROWS), F32),
+            pltpu.VMEM((CTX // 2, TALL, PAIR), F32),
             pltpu.VMEM((CHUNKS, ROWS, WIDE), BF16),
-            dma((2,)), dma, dma, dma, dma, dma((CHUNKS,)), dma((CHUNKS,)),
+            dma((4,)), dma, dma, dma, dma, dma((CHUNKS,)), dma((CHUNKS,)),
             dma((7,)), dma((7,)), dma((CTX,)), dma((CTX,)), dma((CHUNKS,)),
         ],
         compiler_params=pltpu.CompilerParams(
@@ -316,7 +327,7 @@
             flops=8 << 30, bytes_accessed=4 << 20, transcendentals=16 << 20
         ),
         name="relay_attend",
-    )(turns.reshape(1, ROWS), labs.reshape(DP, 1, HD), queries, keys_values.reshape(ROWS, 2 * HD))
+    )(routing.T, documents.reshape(1, ROWS), queries, keys_values.reshape(ROWS, 2, HD))
 
 
 def solution(mesh):

time: 129 us -> 92.4 us (0.72)
  the two profiles are of different devices: /device:TPU:56 before, /device:TPU:25 now
where the time goes in v2:
time: 92.4 us; the launch traced here: 92.3 us
  Pallas kernels  90 us (97%)
  local copies, waits for them, and re-layouts  2.26 us (2%)
    pallas_call x1, Pallas kernels, local(): pl.pallas_call(kernel, out_shape=jax.ShapeDtypeStruct((ROWS, HEADS * HD),...  90 us
    unnamed x1, local copies, waits for them, and re-layouts  2.26 us

profile of v2, /device:TPU:25, one launch (start us, length us, event | category | flops | bytes accessed | tf_op | source)
XLA Modules:
  0.0 92.3 jit_solution(15527827255668320604)
XLA Ops:
  0.0 90.0 %relay_attend.1 = bf16[512,1024]{1,0:T(8,128)(2,1)} custom-call(s32[2,512]{1,0:T(2,128)} %bitcast.4, s32[1,512]{1,0:T(1,128)} %bitcast.5, bf16[512,1024]{1,0:T(8,128)(2,1)} %q_hbm.1, bf16[512,2,128]{2,1,0:T(2,128)(2,1)} %bitcast.3), custom_call_target="tpu_custom_call" | custom-call | flops 8589934592 | bytes 4194304 | tf_op jit(solution)/shard_map/relay_attend/pallas_call | solution.py:296
  90.1 2.3 %copy.6 = bf16[512,1024]{1,0:T(8,128)(2,1)} copy(bf16[512,1024]{1,0:T(8,128)(2,1)} %relay_attend.1) | data formatting | bytes 2097152

commit v3 on v2

--- a/solution.py
+++ b/solution.py
@@ -24,11 +24,11 @@
 
 
 def kernel(
-    route_hbm, doc_hbm, q_hbm, kv_hbm, out_hbm,
+    route_hbm, doc_hbm, q_hbm, kv_hbm, out,
     route_v, doc_v, q_v, kv_v, lab_s, lab_r, kv_s, kv_r, q_s, q_r,
-    spread, gather, begin, k_all, v_all, q_two, scores, out_v,
+    spread, gather, begin, k_all, v_all, q_two, bias, scores,
     in_sem, lab_ss, lab_rs, kv_ss, kv_rs, q_ss, q_rs,
-    k_ss, v_ss, k_rs, v_rs, out_sem,
+    k_ss, v_ss, k_rs, v_rs,
 ):
     me, cx = lax.axis_index("dp"), lax.axis_index("ctx")
     y, low = cx // 2, cx % 2
@@ -112,10 +112,6 @@
 
         lax.fori_loop(1, DP, send_q, 0)
 
-    pack_q(0)
-    send_chunk(0)
-    for ch in range(1, CHUNKS):
-        pack_q(ch)
     others = pl.ds(1, DP - 1)
 
     def group(src, dst, send, recv):
@@ -123,6 +119,16 @@
             src, dst, send, recv, device_id=((me + 1) % DP, cx), device_id_type=MESH
         )
 
+    def kv_group():
+        return group(kv_s.at[others], kv_r.at[others], kv_ss, kv_rs)
+
+    def q_group(ch):
+        return group(q_s.at[ch, others], q_r.at[ch, others], q_ss.at[ch], q_rs.at[ch])
+
+    for ch in range(CHUNKS):
+        pack_q(ch)
+    kv_group().wait_send()
+    send_chunk(0)
     labels = group(lab_s.at[others], lab_r.at[others], lab_ss, lab_rs)
     labels.wait_recv()
     lab = lab_r[:, 0, :]
@@ -154,7 +160,7 @@
     def unpacked(x):
         return jnp.dot(gather[...], x.reshape(slots, x.shape[2]), preferred_element_type=F32)
 
-    group(kv_s.at[others], kv_r.at[others], kv_ss, kv_rs).wait_recv()
+    kv_group().wait_recv()
     own = unpacked(kv_r[...])
     v_all[cx] = own[:, HD:].astype(BF16)
     k_all[cx] = jnp.transpose(own[:, :HD]).astype(BF16)
@@ -168,48 +174,52 @@
             for a, s, r in ((k_all, k_ss, k_rs), (v_all, v_ss, v_rs))
         ]
 
-    ups = [(dy, y + dy < 4, (y + dy) % 4 * 2 + low) for dy in (1, 2, 3)]
+    ups = [(n, n > y, n * 2 + low) for n in (3, 2, 1)]
 
     for c in ctx_copies(0, cx, mate):
         c.start()
 
-    for dy, live, there in ups:
+    for n, live, there in ups:
 
         @pl.when(live)
-        def _(dy=dy, there=there):
-            for c in ctx_copies(dy, cx, there):
+        def _(n=n, there=there):
+            for c in ctx_copies(n, cx, there):
                 c.start()
 
-    send_chunk(1)
     for c in ctx_copies(0, mate, mate):
         c.wait_recv()
 
-    for dy, live, there in ups:
+    for n, live, there in ups:
 
         @pl.when(live)
-        def _(dy=dy, there=there):
-            for c in ctx_copies(3 + dy, mate, there):
+        def _(n=n, there=there):
+            for c in ctx_copies(3 + n, mate, there):
                 c.start()
 
+    send_chunk(1)
+    key_lane = lax.broadcasted_iota(I32, (ROWS, PAIR), 1)
+    query_row = lax.broadcasted_iota(I32, (ROWS, PAIR), 0) + cx * ROWS
+    first = jnp.concatenate([begin[...]] * (PAIR // HD), axis=1)
+
+    def draw_mask(i, _):
+        key_pos = key_lane + (y - i) * PAIR
+        keep = (key_pos >= first) & (key_pos <= query_row)
+        bias[i] = jnp.where(keep, 0.0, NEG)
+        return 0
+
+    lax.fori_loop(0, y + 1, draw_mask, 0)
+    q_group(0).wait_send()
     send_chunk(2)
+    q_group(1).wait_send()
     send_chunk(3)
     ones = jnp.ones((PAIR, HD), BF16)
-    key_lane = lax.broadcasted_iota(I32, (ROWS, PAIR), 1)
-    query_row = lax.broadcasted_iota(I32, (ROWS, PAIR), 0) + low * ROWS
-
-    def score(pair, diagonal):
+    def score(i):
+        pair = y - i
         kt = jnp.concatenate([k_all[2 * pair], k_all[2 * pair + 1]], axis=1)
         s = jnp.dot(
             q_two[...], jnp.concatenate([kt, kt], axis=0), preferred_element_type=F32
         )
-        first = jnp.concatenate([begin[...]] * (PAIR // HD), axis=1)
-        keep = key_lane + pair * PAIR >= first
-        if diagonal:
-            keep = keep & (key_lane <= query_row)
-        parts = [
-            jnp.where(keep, s[h * ROWS : (h + 1) * ROWS], NEG) for h in range(PER)
-        ]
-        return jnp.concatenate(parts, axis=0)
+        return s + jnp.concatenate([bias[i]] * PER, axis=0)
 
     def widest(top, s):
         for i in range(PAIR // HD):
@@ -217,9 +227,7 @@
         return top
 
     def chunk(ch, _):
-        group(
-            q_s.at[ch, others], q_r.at[ch, others], q_ss.at[ch], q_rs.at[ch]
-        ).wait_recv()
+        q_group(ch).wait_recv()
         mine = unpacked(q_r[ch]) * FACTOR
         high = mine.astype(BF16)
         rest = (mine - high.astype(F32)).astype(BF16)
@@ -227,24 +235,22 @@
             at, cols = slice(h * ROWS, (h + 1) * ROWS), slice(h * HD, (h + 1) * HD)
             q_two[at, :HD] = high[:, cols]
             q_two[at, HD:] = rest[:, cols]
-        s = score(y, True)
-        scores[0] = s
-        top = widest(jnp.full((TALL, HD), NEG, F32), s)
-
         def first_pass(i, top):
             pair = y - i
 
-            @pl.when(ch == 0)
+            @pl.when((ch == 0) & (i > 0))
             def _():
                 for block in (2 * pair, 2 * pair + 1):
                     for c in ctx_copies(0, block, mate):
                         c.wait_recv()
 
-            s = score(pair, False)
+            s = score(i)
             scores[i] = s
             return widest(top, s)
 
-        top = lax.fori_loop(1, y + 1, first_pass, top)
+        top = lax.fori_loop(
+            0, y + 1, first_pass, jnp.full((TALL, HD), NEG, F32)
+        )
         peak = jnp.max(top, axis=1, keepdims=True)
 
         def second_pass(i, total):
@@ -257,37 +263,27 @@
         total = lax.fori_loop(0, y + 1, second_pass, jnp.zeros((TALL, 2 * HD), F32))
         done = (total[:, :HD] / total[:, HD:]).astype(BF16)
         for h in range(PER):
-            out_v[ch, :, h * HD : (h + 1) * HD] = done[h * ROWS : (h + 1) * ROWS]
-        put(ch).start()
+            at = pl.ds(pl.multiple_of(ch * WIDE + h * HD, HD), HD)
+            out[:, at] = done[h * ROWS : (h + 1) * ROWS]
         return 0
 
-    def put(ch):
-        at = pl.ds(pl.multiple_of(ch * WIDE, WIDE), WIDE)
-        return pltpu.make_async_copy(out_v.at[ch], out_hbm.at[:, at], out_sem.at[ch])
-
     lax.fori_loop(0, CHUNKS, chunk, 0)
 
     labels.wait_send()
-    group(kv_s.at[others], kv_r.at[others], kv_ss, kv_rs).wait_send()
-    for ch in range(CHUNKS):
-        group(
-            q_s.at[ch, others], q_r.at[ch, others], q_ss.at[ch], q_rs.at[ch]
-        ).wait_send()
+    q_group(2).wait_send()
+    q_group(3).wait_send()
 
     for c in ctx_copies(0, cx, mate):
         c.wait_send()
 
-    for dy, live, there in ups:
+    for n, live, there in ups:
 
         @pl.when(live)
-        def _(dy=dy, there=there):
-            for c in ctx_copies(dy, cx, there):
+        def _(n=n, there=there):
+            for c in ctx_copies(n, cx, there):
                 c.wait_send()
-            for c in ctx_copies(3 + dy, mate, there):
+            for c in ctx_copies(3 + n, mate, there):
                 c.wait_send()
-
-    for ch in range(CHUNKS):
-        put(ch).wait()
 
 
 def local(queries, keys_values, routing, documents):
@@ -295,9 +291,9 @@
     anywhere = pl.BlockSpec(memory_space=pl.ANY)
     return pl.pallas_call(
         kernel,
-        out_shape=jax.ShapeDtypeStruct((ROWS, HEADS * HD), BF16),
+        out_shape=pltpu.VMEM((ROWS, HEADS * HD), BF16),
         in_specs=[anywhere] * 4,
-        out_specs=anywhere,
+        out_specs=pl.BlockSpec(memory_space=pltpu.VMEM),
         scratch_shapes=[
             pltpu.VMEM((2, ROWS), I32),
             pltpu.VMEM((1, ROWS), I32),
@@ -315,10 +311,10 @@
             pltpu.VMEM((CTX, HD, ROWS), BF16),
             pltpu.VMEM((CTX, ROWS, HD), BF16),
             pltpu.VMEM((TALL, 2 * HD), BF16),
+            pltpu.VMEM((CTX // 2, ROWS, PAIR), F32),
             pltpu.VMEM((CTX // 2, TALL, PAIR), F32),
-            pltpu.VMEM((CHUNKS, ROWS, WIDE), BF16),
             dma((4,)), dma, dma, dma, dma, dma((CHUNKS,)), dma((CHUNKS,)),
-            dma((7,)), dma((7,)), dma((CTX,)), dma((CTX,)), dma((CHUNKS,)),
+            dma((7,)), dma((7,)), dma((CTX,)), dma((CTX,)),
         ],
         compiler_params=pltpu.CompilerParams(
             collective_id=1, has_side_effects=True, vmem_limit_bytes=56 << 20

time: 92.4 us -> 85.5 us (0.925)
  Pallas kernels: 90 us -> 83.7 us
  local copies, waits for them, and re-layouts: 2.26 us -> 0.97 us
    pallas_call x1, Pallas kernels: 90 us -> 83.7 us  [local(): pl.pallas_call(kernel, out_shape=pltpu.VMEM((ROWS, HEADS * HD), BF16), in...]
    unnamed x1, local copies, waits for them, and re-layouts: 2.26 us -> 0.97 us
where the time goes in v3:
time: 85.5 us; the launch traced here: 84.7 us
  Pallas kernels  83.7 us (98%)
  local copies, waits for them, and re-layouts  0.97 us (1%)
    pallas_call x1, Pallas kernels, local(): pl.pallas_call(kernel, out_shape=pltpu.VMEM((ROWS, HEADS * HD), BF16), in...  83.7 us

profile of v3, /device:TPU:25, one launch (start us, length us, event | category | flops | bytes accessed | tf_op | source)
XLA Modules:
  0.0 84.7 jit_solution(17382083722090406190)
XLA Ops:
  0.0 83.7 %relay_attend.1 = bf16[512,1024]{1,0:T(8,128)(2,1)S(1)} custom-call(s32[2,512]{1,0:T(2,128)} %bitcast.4, s32[1,512]{1,0:T(1,128)} %bitcast.5, bf16[512,1024]{1,0:T(8,128)(2,1)} %q_hbm.1, bf16[512,2,128]{2,1,0:T(2,128)(2,1)} %bitcast.3), custom_call_target="tpu_custom_call" | custom-call | flops 8589934592 | bytes 4194304 | tf_op jit(solution)/shard_map/relay_attend/pallas_call | solution.py:292
  83.7 1.0 %copy.6 = bf16[512,1024]{1,0:T(8,128)(2,1)} copy(bf16[512,1024]{1,0:T(8,128)(2,1)S(1)} %relay_attend.1) | data formatting | bytes 2097152

commit v4 on v3

--- a/solution.py
+++ b/solution.py
@@ -13,10 +13,11 @@
 DP, CTX = 32, 8
 ROWS, HEADS, HD, CAP = 512, 8, 128, 32
 BLOCKS = ROWS // CAP
-PER = 2
-CHUNKS = HEADS // PER
-WIDE = PER * HD
-TALL = PER * ROWS
+SIZES = (2, 2, 2, 1, 1)
+STARTS = (0, 2, 4, 6, 7)
+MOST = 2
+CHUNKS = len(SIZES)
+SUMS = HD + 16
 PAIR = 2 * ROWS
 SEQ = 4096
 NEG = -1e30
@@ -25,8 +26,8 @@
 
 def kernel(
     route_hbm, doc_hbm, q_hbm, kv_hbm, out,
-    route_v, doc_v, q_v, kv_v, lab_s, lab_r, kv_s, kv_r, q_s, q_r,
-    spread, gather, begin, k_all, v_all, q_two, bias, scores,
+    route_v, doc_v, q_v, kv_v, lab_s, lab_r, kv_s, kv_r, q_s2, q_r2, q_s1, q_r1,
+    spread, gather, begin, k_all, v_all, q_cols, bias, scores,
     in_sem, lab_ss, lab_rs, kv_ss, kv_rs, q_ss, q_rs,
     k_ss, v_ss, k_rs, v_rs,
 ):
@@ -38,7 +39,7 @@
 
     def greet(j, _):
         pl.semaphore_signal(
-            barrier, inc=1, device_id=((me + j) % DP, cx), device_id_type=MESH
+            barrier, inc=1, device_id=((me + j) & (DP - 1), cx), device_id_type=MESH
         )
         return 0
 
@@ -84,7 +85,7 @@
     pl.semaphore_wait(barrier, DP - 1 + 4)
 
     def send_kv(j, _):
-        there = ((me + j) % DP, cx)
+        there = ((me + j) & (DP - 1), cx)
         pltpu.make_async_remote_copy(
             lab_s.at[j], lab_r.at[j], lab_ss, lab_rs, device_id=there, device_id_type=MESH
         ).start()
@@ -98,15 +99,23 @@
     kv_r[0] = kv_s[0]
     gets[3].wait()
 
+    def q_bufs(ch):
+        if SIZES[ch] == 2:
+            return q_s2.at[ch], q_r2.at[ch]
+        return q_s1.at[ch - 3], q_r1.at[ch - 3]
+
     def pack_q(ch):
-        q_s[ch] = packed(q_v[:, ch * WIDE : (ch + 1) * WIDE])
-        q_r[ch, 0] = q_s[ch, 0]
+        held, got = q_bufs(ch)
+        held[...] = packed(q_v[:, STARTS[ch] * HD : (STARTS[ch] + SIZES[ch]) * HD])
+        got[0] = held[0]
 
     def send_chunk(ch):
+        held, got = q_bufs(ch)
+
         def send_q(j, _):
             pltpu.make_async_remote_copy(
-                q_s.at[ch, j], q_r.at[ch, j], q_ss.at[ch], q_rs.at[ch],
-                device_id=((me + j) % DP, cx), device_id_type=MESH,
+                held.at[j], got.at[j], q_ss.at[ch], q_rs.at[ch],
+                device_id=((me + j) & (DP - 1), cx), device_id_type=MESH,
             ).start()
             return 0
 
@@ -123,12 +132,13 @@
         return group(kv_s.at[others], kv_r.at[others], kv_ss, kv_rs)
 
     def q_group(ch):
-        return group(q_s.at[ch, others], q_r.at[ch, others], q_ss.at[ch], q_rs.at[ch])
+        held, got = q_bufs(ch)
+        return group(held.at[others], got.at[others], q_ss.at[ch], q_rs.at[ch])
 
     for ch in range(CHUNKS):
         pack_q(ch)
+    send_chunk(0)
     kv_group().wait_send()
-    send_chunk(0)
     labels = group(lab_s.at[others], lab_r.at[others], lab_ss, lab_rs)
     labels.wait_recv()
     lab = lab_r[:, 0, :]
@@ -155,15 +165,15 @@
     for b in range(BLOCKS):
         row = jnp.sum(jnp.where(place == b + 1, lab // CAP, 0), axis=0, keepdims=True)
         column = jnp.sum(jnp.where(square, row, 0), axis=1, keepdims=True)
-        begin[b * CAP : (b + 1) * CAP, :] = jnp.broadcast_to(column, (CAP, HD))
+        begin[b * CAP : (b + 1) * CAP, :] = jnp.broadcast_to(column.astype(F32), (CAP, HD))
 
     def unpacked(x):
         return jnp.dot(gather[...], x.reshape(slots, x.shape[2]), preferred_element_type=F32)
 
     kv_group().wait_recv()
     own = unpacked(kv_r[...])
-    v_all[cx] = own[:, HD:].astype(BF16)
-    k_all[cx] = jnp.transpose(own[:, :HD]).astype(BF16)
+    k_all[cx] = own[:, :HD].astype(BF16)
+    v_all[cx] = jnp.transpose(own[:, HD:]).astype(BF16)
 
     def ctx_copies(n, block, there):
         return [
@@ -176,105 +186,118 @@
 
     ups = [(n, n > y, n * 2 + low) for n in (3, 2, 1)]
 
-    for c in ctx_copies(0, cx, mate):
-        c.start()
-
-    for n, live, there in ups:
-
-        @pl.when(live)
-        def _(n=n, there=there):
-            for c in ctx_copies(n, cx, there):
-                c.start()
-
+    for a, s, r in ((k_all, k_ss, k_rs), (v_all, v_ss, v_rs)):
+        step_rows = a.shape[1] // 4
+        for i in range(4):
+            piece = a.at[cx, pl.ds(i * step_rows, step_rows)]
+            pltpu.make_async_remote_copy(
+                piece, piece, s.at[0], r.at[cx], device_id=(me, mate), device_id_type=MESH
+            ).start()
+
+    def send_up(base, block):
+        for part in (0, 1):
+            for n, live, there in ups:
+
+                @pl.when(live)
+                def _(n=n, there=there, part=part):
+                    ctx_copies(base + n, block, there)[part].start()
+
+    send_up(0, cx)
     for c in ctx_copies(0, mate, mate):
         c.wait_recv()
 
-    for n, live, there in ups:
-
-        @pl.when(live)
-        def _(n=n, there=there):
-            for c in ctx_copies(3 + n, mate, there):
-                c.start()
-
+    send_up(3, mate)
+    for c in ctx_copies(0, cx, mate):
+        c.wait_send()
     send_chunk(1)
-    key_lane = lax.broadcasted_iota(I32, (ROWS, PAIR), 1)
-    query_row = lax.broadcasted_iota(I32, (ROWS, PAIR), 0) + cx * ROWS
-    first = jnp.concatenate([begin[...]] * (PAIR // HD), axis=1)
+    first = jnp.transpose(begin[...])[0:1, :].astype(I32)
+    last = lax.broadcasted_iota(I32, (1, ROWS), 1) + cx * ROWS
+    key_row = lax.broadcasted_iota(I32, (PAIR, ROWS), 0)
 
     def draw_mask(i, _):
-        key_pos = key_lane + (y - i) * PAIR
-        keep = (key_pos >= first) & (key_pos <= query_row)
+        start = (y - i) * PAIR
+        keep = (key_row >= first - start) & (key_row <= last - start)
         bias[i] = jnp.where(keep, 0.0, NEG)
         return 0
 
     lax.fori_loop(0, y + 1, draw_mask, 0)
     q_group(0).wait_send()
     send_chunk(2)
-    q_group(1).wait_send()
-    send_chunk(3)
-    ones = jnp.ones((PAIR, HD), BF16)
-    def score(i):
-        pair = y - i
-        kt = jnp.concatenate([k_all[2 * pair], k_all[2 * pair + 1]], axis=1)
-        s = jnp.dot(
-            q_two[...], jnp.concatenate([kt, kt], axis=0), preferred_element_type=F32
-        )
-        return s + jnp.concatenate([bias[i]] * PER, axis=0)
-
-    def widest(top, s):
-        for i in range(PAIR // HD):
-            top = jnp.maximum(top, s[:, i * HD : (i + 1) * HD])
-        return top
-
-    def chunk(ch, _):
-        q_group(ch).wait_recv()
-        mine = unpacked(q_r[ch]) * FACTOR
-        high = mine.astype(BF16)
-        rest = (mine - high.astype(F32)).astype(BF16)
-        for h in range(PER):
-            at, cols = slice(h * ROWS, (h + 1) * ROWS), slice(h * HD, (h + 1) * HD)
-            q_two[at, :HD] = high[:, cols]
-            q_two[at, HD:] = rest[:, cols]
+    ones = jnp.ones((SUMS - HD, PAIR), BF16)
+
+    def attend(got, start, size, await_keys):
+        width = size * ROWS
+        mine = unpacked(got) * FACTOR
+        for h in range(size):
+            x = jnp.transpose(mine[:, h * HD : (h + 1) * HD])
+            high = x.astype(BF16)
+            at = slice(h * ROWS, (h + 1) * ROWS)
+            q_cols[:HD, at] = high
+            q_cols[HD:, at] = (x - high.astype(F32)).astype(BF16)
+
+        def await_pair(i, part):
+            @pl.when(await_keys & (i > 0))
+            def _():
+                for block in (2 * (y - i), 2 * (y - i) + 1):
+                    ctx_copies(0, block, mate)[part].wait_recv()
+
         def first_pass(i, top):
             pair = y - i
 
-            @pl.when((ch == 0) & (i > 0))
-            def _():
-                for block in (2 * pair, 2 * pair + 1):
-                    for c in ctx_copies(0, block, mate):
-                        c.wait_recv()
-
-            s = score(i)
-            scores[i] = s
-            return widest(top, s)
-
-        top = lax.fori_loop(
-            0, y + 1, first_pass, jnp.full((TALL, HD), NEG, F32)
-        )
-        peak = jnp.max(top, axis=1, keepdims=True)
+            await_pair(i, 0)
+            k = jnp.concatenate([k_all[2 * pair], k_all[2 * pair + 1]], axis=0)
+            s = jnp.dot(
+                jnp.concatenate([k, k], axis=1), q_cols[:, :width],
+                preferred_element_type=F32,
+            ) + jnp.concatenate([bias[i]] * size, axis=1)
+            scores[i, :, :width] = s
+            return jnp.maximum(top, jnp.max(s.reshape(PAIR // 8, 8, width), axis=0))
+
+        top = lax.fori_loop(0, y + 1, first_pass, jnp.full((8, width), NEG, F32))
+        peak = jnp.max(top, axis=0, keepdims=True)
 
         def second_pass(i, total):
-            w = jnp.exp2(scores[i] - peak).astype(BF16)
             pair = y - i
-            v = jnp.concatenate([v_all[2 * pair], v_all[2 * pair + 1]], axis=0)
-            v = jnp.concatenate([v, ones], axis=1)
-            return total + jnp.dot(w, v, preferred_element_type=F32)
-
-        total = lax.fori_loop(0, y + 1, second_pass, jnp.zeros((TALL, 2 * HD), F32))
-        done = (total[:, :HD] / total[:, HD:]).astype(BF16)
-        for h in range(PER):
-            at = pl.ds(pl.multiple_of(ch * WIDE + h * HD, HD), HD)
-            out[:, at] = done[h * ROWS : (h + 1) * ROWS]
-        return 0
-
-    lax.fori_loop(0, CHUNKS, chunk, 0)
+            await_pair(i, 1)
+            w = jnp.exp2(scores[i, :, :width] - peak).astype(BF16)
+            v = jnp.concatenate([v_all[2 * pair], v_all[2 * pair + 1]], axis=1)
+            v = jnp.concatenate([v, ones], axis=0)
+            return total + jnp.dot(v, w, preferred_element_type=F32)
+
+        total = lax.fori_loop(0, y + 1, second_pass, jnp.zeros((SUMS, width), F32))
+        done = total[:HD] / total[HD : HD + 1]
+        for h in range(size):
+            at = pl.ds(pl.multiple_of((start + h) * HD, HD), HD)
+            out[:, at] = jnp.transpose(done[:, h * ROWS : (h + 1) * ROWS]).astype(BF16)
+
+    def double(ch, _):
+        held, got = q_s2.at[ch], q_r2.at[ch]
+        group(held.at[others], got.at[others], q_ss.at[ch], q_rs.at[ch]).wait_recv()
+
+        @pl.when(ch == 1)
+        def _():
+            send_chunk(3)
+
+        @pl.when(ch == 2)
+        def _():
+            send_chunk(4)
+
+        attend(q_r2[ch], 2 * ch, 2, ch == 0)
+        return 0
+
+    def single(n, _):
+        held, got = q_s1.at[n], q_r1.at[n]
+        group(held.at[others], got.at[others], q_ss.at[n + 3], q_rs.at[n + 3]).wait_recv()
+        attend(q_r1[n], n + 6, 1, n < 0)
+        return 0
+
+    lax.fori_loop(0, 3, double, 0)
+    lax.fori_loop(0, 2, single, 0)
 
     labels.wait_send()
-    q_group(2).wait_send()
-    q_group(3).wait_send()
-
-    for c in ctx_copies(0, cx, mate):
-        c.wait_send()
+    for ch in range(1, CHUNKS):
+        q_group(ch).wait_send()
+
 
     for n, live, there in ups:
 
@@ -303,16 +326,18 @@
             pltpu.VMEM((DP, 1, HD), I32),
             pltpu.VMEM((DP, CAP, 2 * HD), BF16),
             pltpu.VMEM((DP, CAP, 2 * HD), BF16),
-            pltpu.VMEM((CHUNKS, DP, CAP, WIDE), BF16),
-            pltpu.VMEM((CHUNKS, DP, CAP, WIDE), BF16),
+            pltpu.VMEM((3, DP, CAP, 2 * HD), BF16),
+            pltpu.VMEM((3, DP, CAP, 2 * HD), BF16),
+            pltpu.VMEM((2, DP, CAP, HD), BF16),
+            pltpu.VMEM((2, DP, CAP, HD), BF16),
             pltpu.VMEM((DP * CAP, ROWS), BF16),
             pltpu.VMEM((ROWS, DP * CAP), BF16),
-            pltpu.VMEM((ROWS, HD), I32),
+            pltpu.VMEM((ROWS, HD), F32),
+            pltpu.VMEM((CTX, ROWS, HD), BF16),
             pltpu.VMEM((CTX, HD, ROWS), BF16),
-            pltpu.VMEM((CTX, ROWS, HD), BF16),
-            pltpu.VMEM((TALL, 2 * HD), BF16),
-            pltpu.VMEM((CTX // 2, ROWS, PAIR), F32),
-            pltpu.VMEM((CTX // 2, TALL, PAIR), F32),
+            pltpu.VMEM((2 * HD, MOST * ROWS), BF16),
+            pltpu.VMEM((CTX // 2, PAIR, ROWS), F32),
+            pltpu.VMEM((CTX // 2, PAIR, MOST * ROWS), F32),
             dma((4,)), dma, dma, dma, dma, dma((CHUNKS,)), dma((CHUNKS,)),
             dma((7,)), dma((7,)), dma((CTX,)), dma((CTX,)),
         ],

time: 85.5 us -> 84.3 us (0.986)
  no operation moved by 1% of the time
where the time goes in v4:
time: 84.3 us; the launch traced here: 84.2 us
  Pallas kernels  83.2 us (99%)
  local copies, waits for them, and re-layouts  0.97 us (1%)
    pallas_call x1, Pallas kernels, local(): pl.pallas_call(kernel, out_shape=pltpu.VMEM((ROWS, HEADS * HD), BF16), in...  83.2 us

profile of v4, /device:TPU:25, one launch (start us, length us, event | category | flops | bytes accessed | tf_op | source)
XLA Modules:
  0.0 84.2 jit_solution(931479002549747791)
XLA Ops:
  0.0 83.2 %relay_attend.1 = bf16[512,1024]{1,0:T(8,128)(2,1)S(1)} custom-call(s32[2,512]{1,0:T(2,128)} %bitcast.4, s32[1,512]{1,0:T(1,128)} %bitcast.5, bf16[512,1024]{1,0:T(8,128)(2,1)} %q_hbm.1, bf16[512,2,128]{2,1,0:T(2,128)(2,1)} %bitcast.3), custom_call_target="tpu_custom_call" | custom-call | flops 8589934592 | bytes 4194304 | tf_op jit(solution)/shard_map/relay_attend/pallas_call | solution.py:315
  83.3 1.0 %copy.6 = bf16[512,1024]{1,0:T(8,128)(2,1)} copy(bf16[512,1024]{1,0:T(8,128)(2,1)S(1)} %relay_attend.1) | data formatting | bytes 2097152

commit v5 on v4

--- a/solution.py
+++ b/solution.py
@@ -227,13 +227,10 @@
 
     def attend(got, start, size, await_keys):
         width = size * ROWS
-        mine = unpacked(got) * FACTOR
+        mine = unpacked(got)
         for h in range(size):
             x = jnp.transpose(mine[:, h * HD : (h + 1) * HD])
-            high = x.astype(BF16)
-            at = slice(h * ROWS, (h + 1) * ROWS)
-            q_cols[:HD, at] = high
-            q_cols[HD:, at] = (x - high.astype(F32)).astype(BF16)
+            q_cols[:, h * ROWS : (h + 1) * ROWS] = x.astype(BF16)
 
         def await_pair(i, part):
             @pl.when(await_keys & (i > 0))
@@ -241,30 +238,45 @@
                 for block in (2 * (y - i), 2 * (y - i) + 1):
                     ctx_copies(0, block, mate)[part].wait_recv()
 
+        def rate(i, k, top):
+            keys = k.shape[0]
+            s = jnp.dot(k, q_cols[:, :width], preferred_element_type=F32) * FACTOR
+            s = s + jnp.concatenate([bias[i, :keys]] * size, axis=1)
+            scores[i, :keys, :width] = s
+            return jnp.maximum(top, jnp.max(s.reshape(keys // 8, 8, width), axis=0))
+
+        def own_first(n, top):
+            return rate(0, k_all[cx], top)
+
         def first_pass(i, top):
             pair = y - i
-
             await_pair(i, 0)
             k = jnp.concatenate([k_all[2 * pair], k_all[2 * pair + 1]], axis=0)
-            s = jnp.dot(
-                jnp.concatenate([k, k], axis=1), q_cols[:, :width],
-                preferred_element_type=F32,
-            ) + jnp.concatenate([bias[i]] * size, axis=1)
-            scores[i, :, :width] = s
-            return jnp.maximum(top, jnp.max(s.reshape(PAIR // 8, 8, width), axis=0))
-
-        top = lax.fori_loop(0, y + 1, first_pass, jnp.full((8, width), NEG, F32))
+            return rate(i, k, top)
+
+        top = jnp.full((8, width), NEG, F32)
+        top = lax.fori_loop(0, 1 - low, own_first, top)
+        top = lax.fori_loop(1 - low, y + 1, first_pass, top)
         peak = jnp.max(top, axis=0, keepdims=True)
+
+        def add(i, v, total):
+            keys = v.shape[1]
+            w = jnp.exp2(scores[i, :keys, :width] - peak).astype(BF16)
+            v = jnp.concatenate([v, ones[:, :keys]], axis=0)
+            return total + jnp.dot(v, w, preferred_element_type=F32)
+
+        def own_second(n, total):
+            return add(0, v_all[cx], total)
 
         def second_pass(i, total):
             pair = y - i
             await_pair(i, 1)
-            w = jnp.exp2(scores[i, :, :width] - peak).astype(BF16)
             v = jnp.concatenate([v_all[2 * pair], v_all[2 * pair + 1]], axis=1)
-            v = jnp.concatenate([v, ones], axis=0)
-            return total + jnp.dot(v, w, preferred_element_type=F32)
-
-        total = lax.fori_loop(0, y + 1, second_pass, jnp.zeros((SUMS, width), F32))
+            return add(i, v, total)
+
+        total = jnp.zeros((SUMS, width), F32)
+        total = lax.fori_loop(0, 1 - low, own_second, total)
+        total = lax.fori_loop(1 - low, y + 1, second_pass, total)
         done = total[:HD] / total[HD : HD + 1]
         for h in range(size):
             at = pl.ds(pl.multiple_of((start + h) * HD, HD), HD)
@@ -335,7 +347,7 @@
             pltpu.VMEM((ROWS, HD), F32),
             pltpu.VMEM((CTX, ROWS, HD), BF16),
             pltpu.VMEM((CTX, HD, ROWS), BF16),
-            pltpu.VMEM((2 * HD, MOST * ROWS), BF16),
+            pltpu.VMEM((HD, MOST * ROWS), BF16),
             pltpu.VMEM((CTX // 2, PAIR, ROWS), F32),
             pltpu.VMEM((CTX // 2, PAIR, MOST * ROWS), F32),
             dma((4,)), dma, dma, dma, dma, dma((CHUNKS,)), dma((CHUNKS,)),

time: 84.3 us -> 83 us (0.985)
  Pallas kernels: 83.2 us -> 81.9 us
    pallas_call x1, Pallas kernels: 83.2 us -> 81.9 us  [local(): pl.pallas_call(kernel, out_shape=pltpu.VMEM((ROWS, HEADS * HD), BF16), in...]
where the time goes in v5:
time: 83 us; the launch traced here: 82.9 us
  Pallas kernels  81.9 us (99%)
  local copies, waits for them, and re-layouts  0.97 us (1%)
    pallas_call x1, Pallas kernels, local(): pl.pallas_call(kernel, out_shape=pltpu.VMEM((ROWS, HEADS * HD), BF16), in...  81.9 us

profile of v5, /device:TPU:25, one launch (start us, length us, event | category | flops | bytes accessed | tf_op | source)
XLA Modules:
  0.0 82.9 jit_solution(9662376215222593038)
XLA Ops:
  0.0 81.9 %relay_attend.1 = bf16[512,1024]{1,0:T(8,128)(2,1)S(1)} custom-call(s32[2,512]{1,0:T(2,128)} %bitcast.4, s32[1,512]{1,0:T(1,128)} %bitcast.5, bf16[512,1024]{1,0:T(8,128)(2,1)} %q_hbm.1, bf16[512,2,128]{2,1,0:T(2,128)(2,1)} %bitcast.3), custom_call_target="tpu_custom_call" | custom-call | flops 8589934592 | bytes 4194304 | tf_op jit(solution)/shard_map/relay_attend/pallas_call | solution.py:327
  81.9 1.0 %copy.6 = bf16[512,1024]{1,0:T(8,128)(2,1)} copy(bf16[512,1024]{1,0:T(8,128)(2,1)S(1)} %relay_attend.1) | data formatting | bytes 2097152
